TPU v7x, 256 devices: a whole 4x4x8 slice. The times are simulated.
256 devices in a mesh: vir: 64 (over x, z, core), trip: 4 (over y).
Axes of the slice: x: 4, y: 4, z: 8, core: 2. Of those that a mesh axis runs over, the one named last changes fastest.
Arguments:
- triplets: int32 [4, 3], P('trip'), may hold values from 0 to 119, as said below
- pair_integrals: bfloat16 [2, 448, 448, 448], P(None, 'vir'), may hold values from -16 to 16
- k_integrals: bfloat16 [4, 448, 448, 448], P('trip', 'vir'), may hold values from -16 to 16
- pair_amplitudes: bfloat16 [448, 448], replicated, may hold values from -0.25 to 0.25
- k_amplitudes: bfloat16 [4, 2, 448, 448], P('trip'), may hold values from -0.25 to 0.25
- occ_energy: float32 [120], replicated, may hold values from -3 to -0.2
- vir_energy: float32 [448], replicated, may hold values from 0.1 to 1.5
Outputs:
- energies: float32 [4], P('trip')
- vv_density: float32 [448, 448], P('vir')
- vvvo_density: bfloat16 [4, 448, 448, 448], P('trip', 'vir')
Inputs may be any that keep to these rules, and one draw needn't show every extreme that they name: `triplets`: in every row the first two numbers are the same two different occupied orbitals; the third numbers differ from each other and from those two.
All inputs are finite; a program needn't handle non-finite values.
Results may differ from a plain program's by a relative error of at most 0.0052.
Values may be sent and summed in bfloat16 or wider, within the bound.
A program may use at most 128 MiB of HBM per device.

v0:
```python
import jax
import jax.numpy as jnp
from jax import lax
from jax.sharding import PartitionSpec as P


def body(
    triplets, pair_integrals, k_integrals, pair_amplitudes, k_amplitudes, occ_energy, vir_energy
):
    n_local = pair_integrals.shape[1]
    width = pair_integrals.shape[2]
    first = lax.axis_index("vir") * n_local
    vir_local = lax.dynamic_slice_in_dim(vir_energy, first, n_local, 0)
    slab_i = pair_integrals[0]
    slab_j = pair_integrals[1]
    orbital = jnp.arange(occ_energy.shape[0], dtype=jnp.int32)
    row = triplets[0]
    shift = jnp.sum(jnp.where(orbital[None, :] == row[:, None], occ_energy[None, :], 0.0))
    slab_k = k_integrals[0]
    t_ik = k_amplitudes[0, 0]
    t_jk = k_amplitudes[0, 1]
    own = jnp.einsum("acd,bd->abc", slab_i, t_jk, preferred_element_type=jnp.float32)
    own = own + jnp.einsum("abd,dc->abc", slab_i, t_jk, preferred_element_type=jnp.float32)
    b_terms = (
        jnp.einsum("bcd,ad->abc", slab_j, t_ik, preferred_element_type=jnp.float32)
        + jnp.einsum("bad,dc->abc", slab_j, t_ik, preferred_element_type=jnp.float32)
    ).astype(jnp.bfloat16)
    c_terms = (
        jnp.einsum("cbd,ad->abc", slab_k, pair_amplitudes, preferred_element_type=jnp.float32)
        + jnp.einsum("cad,db->abc", slab_k, pair_amplitudes, preferred_element_type=jnp.float32)
    ).astype(jnp.bfloat16)
    b_moved = lax.all_to_all(b_terms, "vir", split_axis=0, concat_axis=1, tiled=True)
    c_moved = lax.all_to_all(c_terms, "vir", split_axis=0, concat_axis=2, tiled=True)
    amplitude = own + b_moved.astype(jnp.float32) + c_moved.astype(jnp.float32)
    denominator = (
        vir_local[:, None, None] + vir_energy[None, :, None] + vir_energy[None, None, :] - shift
    )
    partials = [jnp.sum(amplitude * amplitude / denominator)]
    weighted = (amplitude / denominator).astype(jnp.bfloat16)
    weights = [weighted]
    turned = lax.all_to_all(weighted, "vir", split_axis=2, concat_axis=0, tiled=True)
    gamma = jnp.einsum("ayc,ad->cyd", turned, pair_amplitudes, preferred_element_type=jnp.float32)
    gamma = gamma + jnp.einsum(
        "ybc,db->cyd", turned, pair_amplitudes, preferred_element_type=jnp.float32
    )
    vvvo = [gamma.astype(jnp.bfloat16)]
    energies = lax.psum(jnp.stack(partials), "vir") / float(width) ** 3
    stacked = jnp.stack(weights).reshape(-1, width)
    density_part = lax.psum_scatter(
        lax.dot_general(
            stacked, stacked, (((0,), (0,)), ((), ())), preferred_element_type=jnp.float32
        ),
        "vir",
        scatter_dimension=0,
        tiled=True,
    )
    density = lax.psum(density_part, "trip")
    density = density / float(width * width)
    return (energies, density, jnp.stack(vvvo))


def solution(mesh):
    return jax.shard_map(
        body,
        mesh=mesh,
        in_specs=(
            P("trip", None),
            P(None, "vir", None, None),
            P("trip", "vir", None, None),
            P(),
            P("trip", None, None, None),
            P(),
            P(),
        ),
        out_specs=(P("trip"), P("vir", None), P("trip", "vir", None, None)),
        check_vma=False,
    )
```

profile of v0, /device:TPU:1, one launch (start us, length us, event | category | flops | bytes accessed | tf_op | source)
XLA Modules:
  0.0 630.2 jit_solution(11920397500820100724)
XLA Ops:
  0.6 0.0 copy-start
  0.7 1.9 copy-done
  2.5 2.8 fusion.8
  5.4 2.0 fusion.1
  7.4 3.7 copy.69
  11.1 13.1 %all-to-all-start.1 = ((bf16[448,448,7]{1,2,0:T(8,128)(2,1)}), bf16[448,448,7]{1,2,0:T(8,128)(2,1)}, u32[]{:S(2)}, u32[]{:S(2)}) async-start(bf16[448,448,7]{1,2,0:T(8,128)(2,1)} %copy.69), calls=%async_computation.1 | async-start | bytes 7340032 | tf_op jit(solution)/shard_map/all_to_all | solution.py:33
  24.3 3.8 fusion.12
  28.1 3.8 fusion.2
  32.0 3.6 copy.64
  35.6 73.4 %all-to-all-done.1 = bf16[448,448,7]{1,2,0:T(8,128)(2,1)} async-done(((bf16[448,448,7]{1,2,0:T(8,128)(2,1)}), bf16[448,448,7]{1,2,0:T(8,128)(2,1)}, u32[]{:S(2)}, u32[]{:S(2)}) %all-to-all-start.1) | async-done | bytes 2809888 | tf_op jit(solution)/shard_map/all_to_all | solution.py:33
  108.9 6.1 all-to-all-start
  115.1 0.1 dynamic_slice.3
  115.1 0.7 select_reduce_fusion
  115.8 0.1 broadcast_add_fusion
  115.9 6.3 %fusion.16 = f32[7,448,448]{2,1,0:T(8,128)} fusion(bf16[2,7,448,448]{3,2,1,0:T(8,128)(2,1)} %param.8, bf16[1,2,448,448]{3,2,1,0:T(8,128)(2,1)S(1)} %copy-done.7), kind=kOutput, calls=%fused_computation.21 | convolution fusion | flops 1258815488 | bytes 9289728 | tf_op jit(solution)/shard_map/abd,dc->abc/dot_general | solution.py:23
  122.2 6.0 copy_convert_fusion
  128.2 7.8 %reshape.52 = f32[64,7,448,7]{2,1,0,3:T(8,128)} reshape(f32[448,448,7]{1,0,2:T(8,128)} %copy_convert_fusion) | data formatting | bytes 11239424 | tf_op jit(solution)/shard_map/convert_element_type | solution.py:34
  136.0 9.9 %copy.71 = f32[7,448,64,7]{1,3,2,0:T(8,128)} copy(f32[7,448,64,7]{1,0,2,3:T(8,128)} %bitcast.95) | data formatting | bytes 11239424 | tf_op jit(solution)/shard_map/convert_element_type | solution.py:34
  145.8 7.8 %reshape.50 = f32[7,448,448]{1,2,0:T(8,128)} reshape(f32[7,448,64,7]{1,3,2,0:T(8,128)} %copy.71) | data formatting | bytes 11239424 | tf_op jit(solution)/shard_map/convert_element_type | solution.py:34
  153.6 8.1 %copy.72 = f32[7,448,448]{2,1,0:T(8,128)} copy(f32[7,448,448]{1,2,0:T(8,128)} %reshape.50) | data formatting | bytes 11239424 | tf_op jit(solution)/shard_map/convert_element_type | solution.py:34
  161.7 38.0 %all-to-all-done = bf16[448,7,448]{2,1,0:T(8,128)(2,1)} async-done(((bf16[448,7,448]{2,1,0:T(8,128)(2,1)}), bf16[448,7,448]{2,1,0:T(8,128)(2,1)}, u32[]{:S(2)}, u32[]{:S(2)}) %all-to-all-start) | async-done | bytes 2809888 | tf_op jit(solution)/shard_map/all_to_all | solution.py:32
  199.7 6.0 copy_convert_fusion.1
  205.7 7.8 %reshape.51 = f32[64,7,7,448]{3,1,0,2:T(8,128)} reshape(f32[448,7,448]{2,0,1:T(8,128)} %copy_convert_fusion.1) | data formatting | bytes 11239424 | tf_op jit(solution)/shard_map/convert_element_type | solution.py:34
  213.5 9.9 %copy.66 = f32[7,64,7,448]{3,2,1,0:T(8,128)} copy(f32[7,64,7,448]{3,0,1,2:T(8,128)} %bitcast.96) | data formatting | bytes 11239424 | tf_op jit(solution)/shard_map/convert_element_type | solution.py:34
  223.3 7.8 %reshape.49 = f32[7,448,448]{2,1,0:T(8,128)} reshape(f32[7,64,7,448]{3,2,1,0:T(8,128)} %copy.66) | data formatting | bytes 11239424 | tf_op jit(solution)/shard_map/convert_element_type | solution.py:34
  231.1 10.5 %divide_convert_fusion = (bf16[7,448,448]{2,1,0:T(8,128)(2,1)S(1)}, f32[]{:T(128)}) fusion(f32[]{:T(128)} %select_reduce_fusion, f32[448]{0:T(512)S(1)} %copy-done.8, f32[7,448]{1,0:T(8,128)S(1)} %broadcast_add_fusion, f32[7,448,448]{2,1,0:T(8,128)} %copy.72, f32[7,448,448]{2,1,0:T(8,128)} %reshape.49, f32[7,448,448]{2,1,0:T(8,128)} %fusion.16, ...), kind=kOutput, calls=%fused_computation.8 | convolution fusion | flops 1272864768 | bytes 25762308 | tf_op jit(solution)/shard_map/acd,bd->abc/dot_general | solution.py:22
  241.6 5.7 copy.74
  247.3 5.9 all-to-all-start.2
  253.2 0.0 copy-start.9
  253.2 2.7 convolution_bitcast_fusion
  255.9 200.2 %fusion = f32[8,448]{1,0:T(8,128)S(1)} fusion(f32[448,448]{1,0:T(8,128)} %convolution_bitcast_fusion), kind=kCustom, calls=%all-reduce-scatter | all-reduce-scatter fusion | flops 229377 | bytes 818176
  456.1 1.9 collective-permute-start
  458.0 1.3 collective-permute-start.1
  459.3 1.3 collective-permute-start.7
  460.6 1.3 collective-permute-start.2
  461.9 1.3 collective-permute-start.3
  463.2 1.3 collective-permute-start.4
  464.5 1.3 collective-permute-start.5
  465.8 8.4 %collective-permute-start.6 = (f32[8,448]{1,0:T(8,128)S(1)}, f32[8,448]{1,0:T(8,128)S(1)}, u32[]{:S(2)}, u32[]{:S(2)}) collective-permute-start(f32[8,448]{1,0:T(8,128)S(1)} %fusion), channel_id=1, source_target_pairs={{0,28},{4,32},{8,36},{12,40},{16,44},{20,48},{24,52},{28,56},{32,6... | collective-permute-start | bytes 43016
  474.2 0.6 dynamic-slice.4
  475.5 119.6 %psum.14 = f32[1]{0:T(128)} all-reduce(f32[1]{0:T(128)} %bitcast.18), channel_id=1, replica_groups=mesh['vir'=64,'trip'=4] {'vir'}, use_global_device_ids=true, to_apply=%region_2.3 | all-reduce | flops 1 | bytes 8 | tf_op jit(solution)/shard_map/psum | solution.py:47
  595.7 0.8 concatenate
  596.6 13.4 %psum.15 = f32[7,448]{1,0:T(8,128)S(1)} all-reduce(f32[7,448]{1,0:T(8,128)S(1)} %constant_dynamic-slice_fusion), channel_id=1, replica_groups=mesh['vir'=64,'trip'=4] {'trip'}, use_global_device_ids=true, to_apply=%region_4.5 | all-reduce | flops 3136 | bytes 25088 | tf_op jit(solution)/shard_map/psum | solution.py:57
  610.0 0.6 broadcast_multiply_fusion
  610.6 4.2 copy.76
  614.8 6.4 %all_to_all.32 = bf16[448,448,7]{1,0,2:T(8,128)(2,1)} reshape(bf16[64,7,448,7]{2,1,0,3:T(8,128)(2,1)} %copy.76) | data formatting | bytes 5619712 | tf_op jit(solution)/shard_map/all_to_all | solution.py:41
  621.2 4.0 fusion.34
  625.3 3.7 fusion.7
  (32 shorter events, 0.1 us)
Async XLA Ops:
  0.6 1.9 copy-start
  0.6 4.7 copy-start.3
  7.4 16.9 %copy-start.5 = (bf16[1,2,448,448]{3,2,1,0:T(8,128)(2,1)S(1)}, bf16[1,2,448,448]{3,2,1,0:T(8,128)(2,1)}, u32[]{:S(2)}) copy-start(bf16[1,2,448,448]{3,2,1,0:T(8,128)(2,1)} %param.11) | copy-start | bytes 2408452
  11.1 97.8 %all-to-all-start.1 = ((bf16[448,448,7]{1,2,0:T(8,128)(2,1)}), bf16[448,448,7]{1,2,0:T(8,128)(2,1)}, u32[]{:S(2)}, u32[]{:S(2)}) async-start(bf16[448,448,7]{1,2,0:T(8,128)(2,1)} %copy.69), calls=%async_computation.1 | async-start | bytes 7340032 | tf_op jit(solution)/shard_map/all_to_all | solution.py:33
  24.3 3.8 copy-start.6
  32.0 83.1 %copy-start.8 = (f32[448]{0:T(512)S(1)}, f32[448]{0:T(512)}, u32[]{:S(2)}) copy-start(f32[448]{0:T(512)} %param.13) | copy-start | bytes 5380
  32.0 83.2 %copy-start.10 = (f32[120]{0:T(128)S(1)}, f32[120]{0:T(128)}, u32[]{:S(2)}) copy-start(f32[120]{0:T(128)} %param.12) | copy-start | bytes 1444
  32.0 83.1 %copy-start.11 = (s32[1,3]{1,0:T(1,128)S(1)}, s32[1,3]{1,0:T(1,128)}, u32[]{:S(2)}) copy-start(s32[1,3]{1,0:T(1,128)} %param.7) | copy-start | bytes 40
  35.6 80.3 %copy-start.7 = (bf16[1,2,448,448]{3,2,1,0:T(8,128)(2,1)S(1)}, bf16[1,2,448,448]{3,2,1,0:T(8,128)(2,1)}, u32[]{:S(2)}) copy-start(bf16[1,2,448,448]{3,2,1,0:T(8,128)(2,1)} %param.11) | copy-start | bytes 2408452
  108.9 90.8 %all-to-all-start = ((bf16[448,7,448]{2,1,0:T(8,128)(2,1)}), bf16[448,7,448]{2,1,0:T(8,128)(2,1)}, u32[]{:S(2)}, u32[]{:S(2)}) async-start(bf16[448,7,448]{2,1,0:T(8,128)(2,1)} %copy.64), calls=%async_computation | async-start | bytes 7340032 | tf_op jit(solution)/shard_map/all_to_all | solution.py:32
  247.3 363.3 %all-to-all-start.2 = ((bf16[7,448,448]{1,0,2:T(8,128)(2,1)}), bf16[7,448,448]{1,0,2:T(8,128)(2,1)}, u32[]{:S(2)}, u32[]{:S(2)}) async-start(bf16[7,448,448]{1,0,2:T(8,128)(2,1)} %copy.74), calls=%async_computation.2 | async-start | bytes 7340032 | tf_op jit(solution)/shard_map/all_to_all | solution.py:41
  253.2 221.0 %copy-start.9 = (u32[256]{0:T(256)S(1)}, u32[256]{0:T(256)}, u32[]{:S(2)}) copy-start(u32[256]{0:T(256)} %constant.26) | copy-start | bytes 3076
  456.1 8.4 %collective-permute-start = (f32[8,448]{1,0:T(8,128)S(1)}, f32[8,448]{1,0:T(8,128)S(1)}, u32[]{:S(2)}, u32[]{:S(2)}) collective-permute-start(f32[8,448]{1,0:T(8,128)S(1)} %fusion), channel_id=1, source_target_pairs={{0,4},{4,8},{8,12},{12,16},{16,20},{20,24},{24,28},{28,32},{32,36}... | collective-permute-start | bytes 43016
  458.0 7.8 %collective-permute-start.1 = (f32[8,448]{1,0:T(8,128)S(1)}, f32[8,448]{1,0:T(8,128)S(1)}, u32[]{:S(2)}, u32[]{:S(2)}) collective-permute-start(f32[8,448]{1,0:T(8,128)S(1)} %fusion), channel_id=1, source_target_pairs={{0,8},{4,12},{8,16},{12,20},{16,24},{20,28},{24,32},{28,36},{32,40... | collective-permute-start | bytes 43016
  459.3 3.9 collective-permute-start.7
  460.6 135.1 %collective-permute-start.2 = (f32[8,448]{1,0:T(8,128)S(1)}, f32[8,448]{1,0:T(8,128)S(1)}, u32[]{:S(2)}, u32[]{:S(2)}) collective-permute-start(f32[8,448]{1,0:T(8,128)S(1)} %fusion), channel_id=1, source_target_pairs={{0,12},{4,16},{8,20},{12,24},{16,28},{20,32},{24,36},{28,40},{32,4... | collective-permute-start | bytes 43016
  461.9 133.8 %collective-permute-start.3 = (f32[8,448]{1,0:T(8,128)S(1)}, f32[8,448]{1,0:T(8,128)S(1)}, u32[]{:S(2)}, u32[]{:S(2)}) collective-permute-start(f32[8,448]{1,0:T(8,128)S(1)} %fusion), channel_id=1, source_target_pairs={{0,16},{4,20},{8,24},{12,28},{16,32},{20,36},{24,40},{28,44},{32,4... | collective-permute-start | bytes 43016
  463.2 132.5 %collective-permute-start.4 = (f32[8,448]{1,0:T(8,128)S(1)}, f32[8,448]{1,0:T(8,128)S(1)}, u32[]{:S(2)}, u32[]{:S(2)}) collective-permute-start(f32[8,448]{1,0:T(8,128)S(1)} %fusion), channel_id=1, source_target_pairs={{0,20},{4,24},{8,28},{12,32},{16,36},{20,40},{24,44},{28,48},{32,5... | collective-permute-start | bytes 43016
  464.5 131.2 %collective-permute-start.5 = (f32[8,448]{1,0:T(8,128)S(1)}, f32[8,448]{1,0:T(8,128)S(1)}, u32[]{:S(2)}, u32[]{:S(2)}) collective-permute-start(f32[8,448]{1,0:T(8,128)S(1)} %fusion), channel_id=1, source_target_pairs={{0,24},{4,28},{8,32},{12,36},{16,40},{20,44},{24,48},{28,52},{32,5... | collective-permute-start | bytes 43016
  465.8 129.9 %collective-permute-start.6 = (f32[8,448]{1,0:T(8,128)S(1)}, f32[8,448]{1,0:T(8,128)S(1)}, u32[]{:S(2)}, u32[]{:S(2)}) collective-permute-start(f32[8,448]{1,0:T(8,128)S(1)} %fusion), channel_id=1, source_target_pairs={{0,28},{4,32},{8,36},{12,40},{16,44},{20,48},{24,52},{28,56},{32,6... | collective-permute-start | bytes 43016
  621.2 4.0 copy-start.2
  621.2 4.1 copy-start.4
  621.2 7.8 %copy-start.1 = (bf16[1,7,448,448]{3,2,1,0:T(8,128)(2,1)S(1)}, bf16[1,7,448,448]{3,2,1,0:T(8,128)(2,1)}, u32[]{:S(2)}) copy-start(bf16[1,7,448,448]{3,2,1,0:T(8,128)(2,1)} %param.9) | copy-start | bytes 8429572
where the time goes:
time: 638 us; the launch traced here: 630 us
  blocking collectives  333 us (52%)
  waiting for transfers between devices  111 us (17%)
  local copies, waits for them, and re-layouts  86 us (13%)
  starting transfers between devices  43.2 us (7%)
  matrix products  39.7 us (6%)
  other arithmetic  13.3 us (2%)
    unnamed x1, blocking collectives  200 us
    psum x1, blocking collectives, body(): energies = lax.psum(jnp.stack(partials), 'vir') / float(width) ** 3  120 us
    all_to_all x1, waiting for transfers between devices, body(): lax.all_to_all(c_terms, 'vir', split_axis=0, concat_axis=2, tiled=True)  73.4 us
    convert_element_type x7, local copies, waits for them, and re-layouts, body(): amplitude = own + b_moved.astype(jnp.float32) + c_moved.astype(jnp.float32)  58.9 us
    all_to_all x1, waiting for transfers between devices, body(): lax.all_to_all(b_terms, 'vir', split_axis=0, concat_axis=1, tiled=True)  38 us
    unnamed x8, starting transfers between devices  18 us
    psum x1, blocking collectives, body(): density = lax.psum(density_part, 'trip')  13.4 us
    all_to_all x1, starting transfers between devices, body(): lax.all_to_all(c_terms, 'vir', split_axis=0, concat_axis=2, tiled=True)  13.1 us
  transfers between devices with their start and end apart: 11, of which 2 were waited for; matrix products, arithmetic and copies ran while one was open for 42% of the time, Pallas kernels for 0%

commit v1 on v0

v1 whole, which is shorter than its diff:
```python
import numpy as np
import jax
import jax.numpy as jnp
from jax import lax
from jax.experimental import pallas as pl
from jax.experimental.pallas import tpu as pltpu
from jax.sharding import PartitionSpec as P

MESH = pl.DeviceIdType.MESH
BF, F32 = jnp.bfloat16, jnp.float32
V = 448
N = 64
L = 7
GROUPS = 4
GD = 16
GR = GD * L
SLOT = 64
ROWS_A, ROWS_B = 112, 80
QUARTER = 48


def pack_matrix():
    m = np.zeros((GD, SLOT, L, GD, L), np.float32)
    for p in range(L):
        for q in range(L):
            for j in range(GD):
                m[j, L * p + q, p, j, q] = 1
    m[:, 49] = m[:, 48]
    return m.reshape(GD * SLOT, L * GR)


def unpack_matrix():
    m = np.zeros((L, GD, L, GD, SLOT), np.float32)
    for p in range(L):
        for q in range(L):
            for k in range(GD):
                m[q, k, p, k, L * p + q] = 1
    return m.reshape(L * GR, GD * SLOT)


def row_matrix():
    m = np.zeros((N, 8, N, L), np.float32)
    for j in range(N):
        for i in range(L):
            m[j, i, j, i] = 1
    return m.reshape(N * 8, V)


def nn(x, y):
    return lax.dot_general(x, y, (((1,), (0,)), ((), ())), preferred_element_type=F32)


def nt(x, y):
    return lax.dot_general(x, y, (((1,), (1,)), ((), ())), preferred_element_type=F32)


def tn(x, y):
    return lax.dot_general(x, y, (((0,), (0,)), ((), ())), preferred_element_type=F32)


def iota(shape, dim):
    return lax.broadcasted_iota(jnp.int32, shape, dim)


def packed_a(x, pk):
    o = nn(pk[...], x).reshape(GD, SLOT, 256)
    last = jnp.where(iota((GD, 16, 128), 1) == 0, o[:, 48:64, :128], o[:, 48:64, 128:])
    return o[:, :48, :128].astype(BF), o[:, :48, 128:].astype(BF), last.astype(BF)


def packed_b(x, pk):
    o = nn(pk[...], x).reshape(GD, SLOT, 256)
    row = iota((GD, 32, 128), 1)
    full = jnp.broadcast_to(o[:, 48:49, :128], (GD, 32, 128))
    half = o[:, 32:64, 128:]
    high = jnp.where(row == 30, full, half)
    high = jnp.where(row == 31, full, pltpu.roll(high, 64, 2))
    mixed = jnp.where(iota((GD, 32, 128), 2) < 64, o[:, :32, 128:], high)
    return o[:, :48, :128].astype(BF), mixed.astype(BF)


def spread_a(m0, m1, last, tmp):
    last = last.astype(F32)
    second = jnp.broadcast_to(last[:, 1:2, :], (GD, 16, 128)).astype(BF)
    last = last.astype(BF)
    left = jnp.concatenate([m0, last], axis=1).reshape(GD * SLOT, 128)
    right = jnp.concatenate([m1, second], axis=1).reshape(GD * SLOT, 128)
    tmp[:, 0:128] = left
    tmp[:, 128:256] = right


def spread_b(m0, mixed, tmp):
    mixed = mixed.astype(F32)
    lane = iota((GD, 32, 128), 2) < 64
    turned = pltpu.roll(mixed, 64, 2)
    low = jnp.where(lane, mixed, 0.0).astype(BF)
    high = jnp.where(lane, turned, 0.0).astype(BF)
    row = jnp.where(
        iota((GD, 1, 128), 2) < 64, turned[:, 30:31, :], mixed[:, 31:32, :]
    )
    full = jnp.broadcast_to(row, (GD, 16, 128)).astype(BF)
    left = jnp.concatenate([m0, full], axis=1).reshape(GD * SLOT, 128)
    right = jnp.concatenate([low, high], axis=1).reshape(GD * SLOT, 128)
    tmp[:, 0:128] = left
    tmp[:, 128:256] = right


def kernel(
    trip_ref, occ_ref, virs_ref, vir_ref, pair_hbm, k_hbm, tij, kamp, pk, up, rowm,
    energy_ref, density_ref, vvvo_hbm,
    gi, gj, gk, cs, w, xb, tjt, tit, vrow, tmp,
    g_send, g_recv, sa_send, sa_recv, sb_send, sb_recv, ya_send, ya_recv, yb_send, yb_recv,
    gram, d1, d2, d2s, dfin, out_a,
    ld, g_ss, g_zs, y_ss, y_l, y_r, y_o, a_ss, a_rs, d1_ss, d1_rs, d2_ss, d2_rs, d3_ss, d3_rs,
):
    v = lax.axis_index("vir")
    y = lax.axis_index("trip")
    core = lax.rem(v, 2)
    grp = v // GD
    inner = lax.rem(v, GD)
    chip = v // 2

    load_j = pltpu.make_async_copy(pair_hbm.at[1], gj, ld.at[0])
    load_k = pltpu.make_async_copy(k_hbm.at[0], gk, ld.at[1])
    load_i = pltpu.make_async_copy(pair_hbm.at[0], gi, ld.at[2])
    load_j.start()
    load_k.start()
    load_i.start()

    barrier = pltpu.get_barrier_semaphore()

    def greet(k, c):
        pl.semaphore_signal(
            barrier, inc=1, device_id={"vir": lax.rem(v + k, N), "trip": y}, device_id_type=MESH
        )
        return c

    lax.fori_loop(1, N, greet, 0)
    partner = chip * 2 + (1 - core)
    for dy in (1, 2, 3):
        ty = lax.rem(y + dy, 4)
        pl.semaphore_signal(barrier, inc=1, device_id={"vir": v, "trip": ty}, device_id_type=MESH)
        pl.semaphore_signal(
            barrier, inc=1, device_id={"vir": partner, "trip": ty}, device_id_type=MESH
        )

    tjt[...] = kamp[0, 1].astype(F32).T.astype(BF)
    tit[...] = kamp[0, 0].astype(F32).T.astype(BF)
    vrow[...] = jnp.ones_like(vrow)
    vrow[0:1, 0:V] = vir_ref[...]

    load_j.wait()
    xb[:, :, 384:512] = jnp.zeros((L, V, 128), BF)
    xb[:, :, 0:V] = gj[...]

    def send_group(src, dst, g, ss, rs):
        def one(k, c):
            d = g * GD + lax.rem(inner + k, GD)

            @pl.when(d != v)
            def _():
                pltpu.make_async_remote_copy(
                    src_ref=src.at[d], dst_ref=dst.at[v], send_sem=ss, recv_sem=rs,
                    device_id={"vir": d, "trip": y}, device_id_type=MESH,
                ).start()

            @pl.when(d == v)
            def _():
                pltpu.make_async_copy(src.at[d], dst.at[v], rs).start()

            return c

        lax.fori_loop(0, GD, one, 0)

    def rows_of(g):
        return pl.ds(pl.multiple_of(g * GR, 16), GR)

    def slots_of(g):
        return pl.ds(g * GD, GD)

    def turn(s, c):
        g = lax.rem(grp + s, GROUPS)
        m0, m1, last = packed_a(xb[:, rows_of(g), 0:256].reshape(L * GR, 256), pk)
        g_send[0, slots_of(g)] = m0
        g_send[1, slots_of(g)] = m1
        g_send[2, slots_of(g), 0:16] = last
        m0, mixed = packed_b(xb[:, rows_of(g), 256:512].reshape(L * GR, 256), pk)
        g_send[3, slots_of(g)] = m0
        g_send[2, slots_of(g), 16:48] = mixed

        @pl.when(s == 0)
        def _():
            pl.semaphore_wait(barrier, N - 1 + 6)

        send_group(g_send.at[y], g_recv.at[y], g, g_ss, g_zs.at[grp])
        return c

    lax.fori_loop(0, GROUPS, turn, 0)

    t_ij = tij[...]
    load_k.wait()

    def c_part(c, carry):
        x = gk[c]
        cs[c] = nt(t_ij, x) + nn(x, t_ij)
        return carry

    lax.fori_loop(0, L, c_part, 0)

    up_y, down_y = lax.rem(y + 1, 4), lax.rem(y + 3, 4)

    def y_copy(q, g, ty, rs):
        return pltpu.make_async_remote_copy(
            src_ref=g_recv.at[q, slots_of(g)], dst_ref=g_recv.at[q, slots_of(g)],
            send_sem=y_ss, recv_sem=rs, device_id={"vir": v, "trip": ty}, device_id_type=MESH,
        )

    for s in range(GROUPS):
        g = s
        y_copy(y, g, up_y, g_zs.at[g]).wait_recv()
        y_copy(y, g, up_y, y_l.at[g]).start()
        y_copy(y, g, down_y, y_r.at[g]).start()

    load_i.wait()
    w[:, :, 384:512] = jnp.zeros((L, V, 128), F32)

    def a_part(i, carry):
        x = gi[i]
        w[i, :, 0:V] = nt(x, kamp[0, 1]) + nt(tjt[...], x)
        return carry

    lax.fori_loop(0, L, a_part, 0)

    for g in range(GROUPS):
        y_copy(down_y, g, up_y, y_l.at[g]).wait_recv()
        if g < 2:
            y_copy(down_y, g, up_y, y_o.at[g]).start()
        y_copy(up_y, g, up_y, y_r.at[g]).wait_recv()
        if g >= 2:
            y_copy(up_y, g, down_y, y_o.at[g]).start()
    for g in range(GROUPS):
        y_copy(lax.rem(y + 2, 4), g, up_y, y_o.at[g]).wait_recv()

    def turned(g, c):
        spread_a(
            g_recv[0, slots_of(g)], g_recv[1, slots_of(g)], g_recv[2, slots_of(g), 0:16], tmp
        )
        o = nn(up[...], tmp[...])
        gj[:, rows_of(g), 0:256] = o.reshape(L, GR, 256).astype(BF)
        spread_b(g_recv[3, slots_of(g)], g_recv[2, slots_of(g), 16:48], tmp)
        o = nn(up[...], tmp[...])
        gj[:, rows_of(g), 256:V] = o.reshape(L, GR, 256)[:, :, 0:192].astype(BF)
        return c

    lax.fori_loop(0, GROUPS, turned, 0)

    def send_a(src, dst, n):
        def step(s, c):
            g = lax.rem(grp + s, GROUPS)
            m0, m1, last = packed_a(xb[:, rows_of(g), 0:256].reshape(L * GR, 256), pk)
            src[slots_of(g), 0:48] = m0
            src[slots_of(g), 48:96] = m1
            src[slots_of(g), 96:112] = last
            send_group(src, dst, g, a_ss.at[n], a_rs.at[n])
            return c

        lax.fori_loop(0, GROUPS, step, 0)

    def send_b(src, dst, n):
        def step(s, c):
            g = lax.rem(grp + s, GROUPS)
            m0, mixed = packed_b(xb[:, rows_of(g), 256:512].reshape(L * GR, 256), pk)
            src[slots_of(g), 0:48] = m0
            src[slots_of(g), 48:80] = mixed
            send_group(src, dst, g, a_ss.at[n], a_rs.at[n])
            return c

        lax.fori_loop(0, GROUPS, step, 0)

    def all_of(src, dst, n):
        return pltpu.make_async_remote_copy(
            src_ref=src, dst_ref=dst, send_sem=a_ss.at[n], recv_sem=a_rs.at[n],
            device_id={"vir": lax.rem(v + 1, N), "trip": y}, device_id_type=MESH,
        )

    def s_a(c, carry):
        xb[c, :, 0:256] = (cs[c, :, 0:256] + nt(kamp[0, 0], gj[c, 0:256])).astype(BF)
        return carry

    lax.fori_loop(0, L, s_a, 0)
    send_a(sa_send, sa_recv, 0)

    def s_b(c, carry):
        xb[c, :, 256:V] = (cs[c, :, 256:V] + nt(kamp[0, 0], gj[c, 256:V])).astype(BF)
        return carry

    lax.fori_loop(0, L, s_b, 0)
    send_b(sb_send, sb_recv, 1)

    def b_part(i, carry):
        w[i, :, 0:V] = w[i, :, 0:V] + nt(tit[...], gj[i])
        return carry

    lax.fori_loop(0, L, b_part, 0)

    shift = occ_ref[trip_ref[0, 0]] + occ_ref[trip_ref[0, 1]] + occ_ref[trip_ref[0, 2]]
    vcol = jnp.sum(
        jnp.where(iota((V, V), 0) == iota((V, V), 1), vrow[0:1, 0:V], 0.0), axis=1, keepdims=True
    )

    def weigh(lanes, e):
        def one(i, e):
            x = w[i, :, lanes]
            den = vcol + (vrow[0:1, lanes] + (virs_ref[v * L + i] - shift))
            z = x / den
            xb[i, :, lanes] = z.astype(BF)
            return e + jnp.sum(x * z, axis=0, keepdims=True)

        return lax.fori_loop(0, L, one, e)

    all_of(sa_send, sa_recv, 0).wait_recv()

    def add_a(g, c):
        spread_a(
            sa_recv[slots_of(g), 0:48], sa_recv[slots_of(g), 48:96], sa_recv[slots_of(g), 96:112],
            tmp,
        )
        o = nn(up[...], tmp[...]).reshape(L, GR, 256)
        w[:, rows_of(g), 0:256] = w[:, rows_of(g), 0:256] + o
        return c

    lax.fori_loop(0, GROUPS, add_a, 0)
    e = weigh(slice(0, 256), jnp.zeros((1, 256), F32))
    send_a(ya_send, ya_recv, 2)

    def gram_a(i, acc):
        x = xb[i, :, 0:256]
        return acc + nt(x, x)

    cs[0] = lax.fori_loop(0, L, gram_a, jnp.zeros((V, V), F32))

    all_of(sb_send, sb_recv, 1).wait_recv()

    def add_b(g, c):
        spread_b(sb_recv[slots_of(g), 0:48], sb_recv[slots_of(g), 48:80], tmp)
        o = nn(up[...], tmp[...]).reshape(L, GR, 256)
        w[:, rows_of(g), 256:512] = w[:, rows_of(g), 256:512] + o
        return c

    lax.fori_loop(0, GROUPS, add_b, 0)
    e = weigh(slice(256, 512), e)
    send_b(yb_send, yb_recv, 3)

    def gram_b(i, acc):
        x = xb[i, :, 256:512]
        return acc + nt(x, x)

    total = lax.fori_loop(0, L, gram_b, cs[0])

    hi = total.astype(BF)
    rest = total - hi.astype(F32)
    mid = rest.astype(BF)
    lo = (rest - mid.astype(F32)).astype(BF)
    rows = nn(rowm[...], hi) + nn(rowm[...], mid) + nn(rowm[...], lo)
    energy = jnp.sum(e)
    gram[:, 384:512] = jnp.zeros((N * 8, 128), F32)
    gram[:, 0:V] = rows
    spare = lax.rem(iota((N * 8, 128), 0), 8) == 7
    mine = spare & (iota((N * 8, 128), 1) == y)
    gram[:, 0:128] = jnp.where(mine, energy, gram[:, 0:128])

    piece = y * 2 + core

    def piece_copy(k):
        to = lax.rem(piece + k, 8)
        return pltpu.make_async_remote_copy(
            src_ref=gram.at[pl.ds(pl.multiple_of(to * 64, 64), 64)], dst_ref=d1.at[piece],
            send_sem=d1_ss, recv_sem=d1_rs,
            device_id={"vir": chip * 2 + lax.rem(to, 2), "trip": to // 2}, device_id_type=MESH,
        )

    for k in range(1, 8):
        piece_copy(k).start()
    pltpu.make_async_copy(
        gram.at[pl.ds(pl.multiple_of(piece * 64, 64), 64)], d1.at[piece], d1_rs
    ).start()

    all_of(ya_send, ya_recv, 2).wait_recv()

    def take_a(g, c):
        spread_a(
            ya_recv[slots_of(g), 0:48], ya_recv[slots_of(g), 48:96], ya_recv[slots_of(g), 96:112],
            tmp,
        )
        o = nn(up[...], tmp[...]).reshape(L, GR, 256)
        gk[:, rows_of(g), 0:256] = o.astype(BF)
        return c

    lax.fori_loop(0, GROUPS, take_a, 0)

    def out_first(c, carry):
        x = gk[c, :, 0:256]
        cs[c] = nt(x, tij[:, 0:256])
        cs[c, 0:256] = cs[c, 0:256] + tn(x, tij[...])
        return carry

    lax.fori_loop(0, L, out_first, 0)

    pltpu.make_async_copy(d1, d1, d1_rs).wait()
    d2s[...] = jnp.sum(d1[...], axis=0)

    def owner_send(o, c):
        to = piece * 8 + o
        src = d2s.at[pl.ds(pl.multiple_of(o * 8, 8), 8)]

        @pl.when(to != v)
        def _():
            pltpu.make_async_remote_copy(
                src_ref=src, dst_ref=d2.at[chip], send_sem=d2_ss, recv_sem=d2_rs,
                device_id={"vir": to, "trip": y}, device_id_type=MESH,
            ).start()

        @pl.when(to == v)
        def _():
            pltpu.make_async_copy(src, d2.at[chip], d2_rs).start()

        return c

    lax.fori_loop(0, 8, owner_send, 0)

    is_owner = y == grp

    def fin_copy(ty):
        return pltpu.make_async_remote_copy(
            src_ref=dfin, dst_ref=dfin, send_sem=d3_ss, recv_sem=d3_rs,
            device_id={"vir": v, "trip": ty}, device_id_type=MESH,
        )

    @pl.when(is_owner)
    def _():
        pltpu.make_async_copy(d2, d2, d2_rs).wait()
        dfin[...] = jnp.sum(d2[...], axis=0)
        for dy in (1, 2, 3):
            fin_copy(lax.rem(y + dy, 4)).start()

    all_of(yb_send, yb_recv, 3).wait_recv()

    def take_b(g, c):
        spread_b(yb_recv[slots_of(g), 0:48], yb_recv[slots_of(g), 48:80], tmp)
        o = nn(up[...], tmp[...]).reshape(L, GR, 256)
        gk[:, rows_of(g), 256:V] = o[:, :, 0:192].astype(BF)
        return c

    lax.fori_loop(0, GROUPS, take_b, 0)

    def out_last(c, carry):
        x = gk[c, :, 256:V]
        acc = cs[c] + nt(x, tij[:, 256:V])
        gi[c, 0:256] = acc[0:256].astype(BF)
        gi[c, 256:V] = (acc[256:V] + tn(x, tij[...])).astype(BF)
        pltpu.make_async_copy(gi.at[c], vvvo_hbm.at[0, c], ld.at[0]).start()
        return carry

    lax.fori_loop(0, L, out_last, 0)

    @pl.when(jnp.logical_not(is_owner))
    def _():
        fin_copy(y).wait_recv()

    density_ref[...] = dfin[0:7, 0:V] * (1.0 / (V * V))
    sel = iota((1, 128), 1) == y
    es = jnp.sum(jnp.where(sel, dfin[7:8, 0:128], 0.0), axis=1, keepdims=True)
    energy_ref[...] = jnp.broadcast_to(es * (1.0 / V**3), (8, 128))

    pltpu.make_async_copy(gi, vvvo_hbm.at[0], ld.at[0]).wait()
    pltpu.make_async_remote_copy(
        src_ref=g_recv.at[y, pl.ds(0, N - 1)], dst_ref=g_recv.at[y, pl.ds(0, N - 1)],
        send_sem=g_ss, recv_sem=g_ss, device_id={"vir": v, "trip": up_y}, device_id_type=MESH,
    ).wait_send()
    pltpu.make_async_remote_copy(
        src_ref=g_recv.at[pl.ds(0, 3)], dst_ref=g_recv.at[pl.ds(0, 3)],
        send_sem=y_ss, recv_sem=y_ss, device_id={"vir": v, "trip": up_y}, device_id_type=MESH,
    ).wait_send()
    for n, buf in enumerate((sa_send, sb_send, ya_send, yb_send)):
        part = buf.at[pl.ds(0, N - 1)]
        all_of(part, part, n).wait_send()
    part = d1.at[pl.ds(0, 7)]
    pltpu.make_async_remote_copy(
        src_ref=part, dst_ref=part, send_sem=d1_ss, recv_sem=d1_ss,
        device_id={"vir": v, "trip": up_y}, device_id_type=MESH,
    ).wait_send()

    def drain_owner(count):
        q = d2.at[pl.ds(0, count)]
        pltpu.make_async_remote_copy(
            src_ref=q, dst_ref=q, send_sem=d2_ss, recv_sem=d2_ss,
            device_id={"vir": v, "trip": up_y}, device_id_type=MESH,
        ).wait_send()

    own_piece = (v // 8) == piece

    @pl.when(own_piece)
    def _():
        drain_owner(7)

    @pl.when(jnp.logical_not(own_piece))
    def _():
        drain_owner(8)

    @pl.when(is_owner)
    def _():
        for dy in (1, 2, 3):
            fin_copy(lax.rem(y + dy, 4)).wait_send()


def body(triplets, pair_integrals, k_integrals, pair_amplitudes, k_amplitudes, occ_energy, vir_energy):
    vm = pl.BlockSpec(memory_space=pltpu.VMEM)
    sm = pl.BlockSpec(memory_space=pltpu.SMEM)
    hbm = pl.BlockSpec(memory_space=pl.ANY)
    slab = pltpu.VMEM((L, V, V), BF)
    dma = pltpu.SemaphoreType.DMA
    energy, density, vvvo = pl.pallas_call(
        kernel,
        out_shape=(
            jax.ShapeDtypeStruct((8, 128), F32),
            jax.ShapeDtypeStruct((L, V), F32),
            jax.ShapeDtypeStruct((1, L, V, V), BF),
        ),
        in_specs=[sm, sm, sm, vm, hbm, hbm, vm, vm, vm, vm, vm],
        out_specs=(vm, vm, hbm),
        scratch_shapes=[
            slab, slab, slab,
            pltpu.VMEM((L, V, V), F32),
            pltpu.VMEM((L, V, 512), F32),
            pltpu.VMEM((L, V, 512), BF),
            pltpu.VMEM((V, V), BF),
            pltpu.VMEM((V, V), BF),
            pltpu.VMEM((8, 512), F32),
            pltpu.VMEM((GD * SLOT, 256), BF),
            pltpu.VMEM((4, N, QUARTER, 128), BF),
            pltpu.VMEM((4, N, QUARTER, 128), BF),
            pltpu.VMEM((N, ROWS_A, 128), BF),
            pltpu.VMEM((N, ROWS_A, 128), BF),
            pltpu.VMEM((N, ROWS_B, 128), BF),
            pltpu.VMEM((N, ROWS_B, 128), BF),
            pltpu.VMEM((N, ROWS_A, 128), BF),
            pltpu.VMEM((N, ROWS_A, 128), BF),
            pltpu.VMEM((N, ROWS_B, 128), BF),
            pltpu.VMEM((N, ROWS_B, 128), BF),
            pltpu.VMEM((N * 8, 512), F32),
            pltpu.VMEM((8, 64, 512), F32),
            pltpu.VMEM((32, 8, 512), F32),
            pltpu.VMEM((64, 512), F32),
            pltpu.VMEM((8, 512), F32),
            pltpu.VMEM((8, 128), F32),
            dma((3,)), dma, dma((4,)), dma, dma((4,)), dma((4,)), dma((4,)),
            dma((4,)), dma((4,)), dma, dma, dma, dma, dma, dma,
        ],
        compiler_params=pltpu.CompilerParams(
            collective_id=0, has_side_effects=True, vmem_limit_bytes=60 * 1024 * 1024
        ),
        name="triples",
    )(
        triplets, occ_energy, vir_energy, vir_energy.reshape(1, V), pair_integrals, k_integrals,
        pair_amplitudes, k_amplitudes,
        jnp.asarray(pack_matrix(), BF), jnp.asarray(unpack_matrix(), BF), jnp.asarray(row_matrix(), BF),
    )
    return energy[0, 0:1], density, vvvo


def solution(mesh):
    return jax.shard_map(
        body,
        mesh=mesh,
        in_specs=(
            P("trip", None),
            P(None, "vir", None, None),
            P("trip", "vir", None, None),
            P(),
            P("trip", None, None, None),
            P(),
            P(),
        ),
        out_specs=(P("trip"), P("vir", None), P("trip", "vir", None, None)),
        check_vma=False,
    )
```

time: 638 us -> 227 us (0.36); the launches traced: 630 us -> 227 us
  blocking collectives: 333 us -> 0 us
  Pallas kernels: 0 us -> 220 us
  waiting for transfers between devices: 111 us -> 0 us
  local copies, waits for them, and re-layouts: 86 us -> 6.41 us
  starting transfers between devices: 43.2 us -> 0 us
  matrix products: 39.7 us -> 0 us
  other arithmetic: 13.3 us -> 0 us
    pallas_call x0 -> x1, Pallas kernels: none -> 220 us  [body(): pl.pallas_call(kernel, out_shape=(jax.ShapeDtypeStruct((8, 128), F32), ja...]
    unnamed x1 -> x0, blocking collectives: 200 us -> none
    psum x2 -> x0, blocking collectives: 133 us -> none  [the longest x1 120 us: body(): energies = lax.psum(jnp.stack(partials), 'vir') / float(width) ** 3]
    all_to_all x3 -> x0, waiting for transfers between devices: 111 us -> none  [the longest x1 73.4 us: body(): lax.all_to_all(c_terms, 'vir', split_axis=0, concat_axis=2, tiled=True)]
    convert_element_type x10 -> x0, local copies, waits for them, and re-layouts: 71.9 us -> none  [the longest x7 58.9 us: body(): amplitude = own + b_moved.astype(jnp.float32) + c_moved.astype(jnp.float32)]
    dot_general x9 -> x0, matrix products: 39.7 us -> none  [the longest x1 10.5 us: body(): jnp.einsum('acd,bd->abc', slab_i, t_jk, preferred_element_type=jnp.float32)]
    all_to_all x3 -> x0, starting transfers between devices: 25.1 us -> none  [the longest x1 13.1 us: body(): lax.all_to_all(c_terms, 'vir', split_axis=0, concat_axis=2, tiled=True)]
    unnamed x8 -> x0, starting transfers between devices: 18 us -> none
  transfers between devices with their start and end apart: 11 -> 0, of which waited for: 2 -> 0; matrix products, arithmetic and copies ran while one was open for 42% -> 0% of each run, Pallas kernels for 0% -> 0%
where the time goes in v1:
time: 227 us
  Pallas kernels  220 us (97%)
  local copies, waits for them, and re-layouts  6.41 us (3%)
    pallas_call x1, Pallas kernels, body(): pl.pallas_call(kernel, out_shape=(jax.ShapeDtypeStruct((8, 128), F32), ja...  220 us
    unnamed x2, local copies, waits for them, and re-layouts  5.22 us

profile of v1, /device:TPU:1, one launch (start us, length us, event | category | flops | bytes accessed | tf_op | source)
XLA Modules:
  0.0 226.7 jit_solution(13093073116314210410)
XLA Ops:
  0.6 219.7 %triples.1 = (f32[8,128]{1,0:T(8,128)}, f32[7,448]{1,0:T(8,128)}, bf16[1,7,448,448]{3,2,1,0:T(8,128)(2,1)}) custom-call(s32[1,3]{1,0:T(1,128)} %trip_ref.1, f32[120]{0:T(128)} %occ_ref.1, f32[448]{0:T(512)} %virs_ref.1, f32[1,448]{1,0:T(1,128)} %bitcast.2, bf16[2,7,448,448]{3,2,1,0:T(8,128)(2,1)} %pair_hbm.1, bf16[1,7,448,448]{3,2,1,0:T(8,128)(2,1)} %k_hbm.1, ...), custom_call_target="tpu_custom_call" | custom-call | tf_op jit(solution)/shard_map/triples/pallas_call | solution.py:522
  220.3 1.2 slice.3
  221.5 1.3 copy.15
  222.8 3.9 %copy.16 = bf16[1,7,448,448]{3,2,1,0:T(8,128)(2,1)} copy(bf16[1,7,448,448]{3,2,1,0:T(8,128)(2,1)} %get-tuple-element.14) | data formatting | bytes 5619712

commit v2 on v1

v2 whole, which is shorter than its diff:
```python
import numpy as np
import jax
import jax.numpy as jnp
from jax import lax
from jax.experimental import pallas as pl
from jax.experimental.pallas import tpu as pltpu
from jax.sharding import PartitionSpec as P

MESH = pl.DeviceIdType.MESH
BF, F32 = jnp.bfloat16, jnp.float32
V = 448
N = 64
L = 7
GROUPS = 4
GD = 16
GR = GD * L
SLOT = 64
ROWS_A, ROWS_B = 96, 80


def pack_matrix():
    m = np.zeros((GD, SLOT, L, GD, L), np.float32)
    for p in range(L):
        for q in range(L):
            for j in range(GD):
                m[j, L * p + q, p, j, q] = 1
    return m.reshape(GD * SLOT, L * GR)


def unpack_matrix():
    m = np.zeros((L, GD, L, GD, SLOT), np.float32)
    for p in range(L):
        for q in range(L):
            for k in range(GD):
                m[q, k, p, k, L * p + q] = 1
    return m.reshape(L * GR, GD * SLOT)


def pack_last():
    m = np.zeros((GD, 8, GD, L), np.float32)
    for j in range(GD):
        m[j, :, j, L - 1] = 1
    return m.reshape(GD * 8, GR)


def unpack_last():
    m = np.zeros((GD, L, GD, 8), np.float32)
    for j in range(GD):
        m[j, L - 1, j, 0] = 1
    return m.reshape(GR, GD * 8)


def row_matrix():
    m = np.zeros((N, 8, N, L), np.float32)
    for j in range(N):
        for i in range(L):
            m[j, i, j, i] = 1
    return m.reshape(N * 8, V)


def nn(x, y):
    return lax.dot_general(x, y, (((1,), (0,)), ((), ())), preferred_element_type=F32)


def nt(x, y):
    return lax.dot_general(x, y, (((1,), (1,)), ((), ())), preferred_element_type=F32)


def tn(x, y):
    return lax.dot_general(x, y, (((0,), (0,)), ((), ())), preferred_element_type=F32)


def iota(shape, dim):
    return lax.broadcasted_iota(jnp.int32, shape, dim)


def packed_a(x, pk):
    o = nn(pk[...], x).reshape(GD, SLOT, 256)
    return o[:, :48, :128].astype(BF), o[:, :48, 128:].astype(BF)


def packed_b(x, last, pk, pl_ref):
    o = nn(pk[...], x).reshape(GD, SLOT, 256)
    t = nn(pl_ref[...], last).reshape(GD, 8, 256)
    shape = (GD, 32, 128)
    row = iota(shape, 1)
    r0 = jnp.broadcast_to(t[:, 0:1, :128], shape)
    r1 = jnp.broadcast_to(t[:, 0:1, 128:], shape)
    r2 = jnp.broadcast_to(o[:, 48:49, :128], shape)
    high = jnp.where(row == 24, r0, jnp.where(row == 26, r1, jnp.where(row == 30, r2, o[:, 32:64, 128:])))
    high = pltpu.roll(high, 64, 2)
    high = jnp.where(row == 25, r0, jnp.where(row == 27, r1, jnp.where(row == 31, r2, high)))
    mixed = jnp.where(iota(shape, 2) < 64, o[:, :32, 128:], high)
    return o[:, :48, :128].astype(BF), mixed.astype(BF)


def spread_a(m0, m1, tmp):
    zero = jnp.zeros((GD, 16, 128), BF)
    tmp[:, 0:128] = jnp.concatenate([m0, zero], axis=1).reshape(GD * SLOT, 128)
    tmp[:, 128:256] = jnp.concatenate([m1, zero], axis=1).reshape(GD * SLOT, 128)


def spread_b(m0, mixed, tmp):
    mixed = mixed.astype(F32)
    lane = iota((GD, 32, 128), 2) < 64
    turned = pltpu.roll(mixed, 64, 2)
    low = jnp.where(lane, mixed, 0.0).astype(BF)
    high = jnp.where(lane, turned, 0.0).astype(BF)

    def joined(k, rows):
        row = jnp.where(
            iota((GD, 1, 128), 2) < 64, turned[:, k : k + 1, :], mixed[:, k + 1 : k + 2, :]
        )
        return jnp.broadcast_to(row, (GD, rows, 128))

    full = joined(30, 16).astype(BF)
    tmp[:, 0:128] = jnp.concatenate([m0, full], axis=1).reshape(GD * SLOT, 128)
    tmp[:, 128:256] = jnp.concatenate([low, high], axis=1).reshape(GD * SLOT, 128)
    return jnp.concatenate(
        [joined(24, 8).reshape(GD * 8, 128), joined(26, 8).reshape(GD * 8, 128)], axis=1
    ).astype(BF)


def kernel(
    trip_ref, occ_ref, virs_ref, vir_ref, pair_hbm, k_hbm, tij_hbm, kamp_hbm, pk_hbm, up_hbm, row_hbm, plast, ulast,
    energy_ref, density_ref, vvvo_hbm,
    gi, gj, gk, tij, kamp, pk, up, rowm, cs, w, xb, tjt, tit, vrow, tmp,
    g_send, g_recv, sa_send, sa_recv, sb_send, sb_recv, ya_send, ya_recv, yb_send, yb_recv,
    gram, d1, d2, d2s, dfin,
    ld, g_ss, g_zs, y_ss, y_fs, y_l, y_r, y_o, a_ss, a_rs, d1_ss, d1_rs, d2_ss, d2_rs, d3_ss, d3_rs,
):
    v = lax.axis_index("vir")
    y = lax.axis_index("trip")
    core = lax.rem(v, 2)
    grp = v // GD
    inner = lax.rem(v, GD)
    chip = v // 2

    loads = [
        pltpu.make_async_copy(src, dst, ld.at[n])
        for n, (src, dst) in enumerate(
            (
                (pk_hbm, pk), (pair_hbm.at[1], gj), (k_hbm.at[0], gk), (tij_hbm, tij),
                (pair_hbm.at[0], gi), (kamp_hbm, kamp), (up_hbm, up), (row_hbm, rowm),
            )
        )
    ]
    for n in range(2):
        loads[n].start()

    barrier = pltpu.get_barrier_semaphore()

    def greet(k, c):
        pl.semaphore_signal(
            barrier, inc=1, device_id={"vir": lax.rem(v + k, N), "trip": y}, device_id_type=MESH
        )
        return c

    lax.fori_loop(1, N, greet, 0)
    partner = chip * 2 + (1 - core)
    for dy in (1, 2, 3):
        ty = lax.rem(y + dy, 4)
        pl.semaphore_signal(barrier, inc=1, device_id={"vir": v, "trip": ty}, device_id_type=MESH)
        pl.semaphore_signal(
            barrier, inc=1, device_id={"vir": partner, "trip": ty}, device_id_type=MESH
        )

    for n in range(2):
        loads[n].wait()
    for n in range(2, 8):
        loads[n].start()

    def send_group(src, dst, g, ss, rs):
        def one(k, c):
            d = g * GD + lax.rem(inner + k, GD)

            @pl.when(d != v)
            def _():
                pltpu.make_async_remote_copy(
                    src_ref=src.at[d], dst_ref=dst.at[v], send_sem=ss, recv_sem=rs,
                    device_id={"vir": d, "trip": y}, device_id_type=MESH,
                ).start()

            @pl.when(d == v)
            def _():
                pltpu.make_async_copy(src.at[d], dst.at[v], rs).start()

            return c

        lax.fori_loop(0, GD, one, 0)

    def rows_of(g):
        return pl.ds(pl.multiple_of(g * GR, 16), GR)

    def slots_of(g):
        return pl.ds(g * GD, GD)

    def turn(s, c):
        g = lax.rem(grp + s, GROUPS)
        x = gj[:, rows_of(g), 0:256].reshape(L * GR, 256)
        m0, m1 = packed_a(x, pk)
        g_send[0, slots_of(g)] = m0
        g_send[1, slots_of(g)] = m1
        z = jnp.concatenate([gj[:, rows_of(g), 256:V], jnp.zeros((L, GR, 64), BF)], axis=2)
        m0, mixed = packed_b(z.reshape(L * GR, 256), gj[L - 1, rows_of(g), 0:256], pk, plast)
        g_send[3, slots_of(g)] = m0
        g_send[2, slots_of(g), 0:32] = mixed

        @pl.when(s == 0)
        def _():
            pl.semaphore_wait(barrier, N - 1 + 6)

        @pl.when(y != 2)
        def _():
            send_group(g_send.at[y], g_recv.at[y], g, g_ss, g_zs.at[grp])

        @pl.when(y == 2)
        def _():
            send_group(
                g_send.at[2, :, pl.ds(0, 32)], g_recv.at[2, :, pl.ds(0, 32)], g, g_ss, g_zs.at[grp]
            )

        return c

    lax.fori_loop(0, GROUPS, turn, 0)

    up_y, down_y = lax.rem(y + 1, 4), lax.rem(y + 3, 4)
    far_y = lax.rem(y + 2, 4)

    def by_size(q, act):
        @pl.when(q != 2)
        def _():
            act(48)

        @pl.when(q == 2)
        def _():
            act(32)

    def y_copy(q, s, rows, ty, rs, ss=None):
        g = lax.rem(grp + GROUPS - s, GROUPS)
        piece = g_recv.at[q, slots_of(g), pl.ds(0, rows)]
        return pltpu.make_async_remote_copy(
            src_ref=piece, dst_ref=piece,
            send_sem=y_ss.at[s] if ss is None else ss, recv_sem=rs,
            device_id={"vir": v, "trip": ty}, device_id_type=MESH,
        )

    def z_step(s):
        g = lax.rem(grp + GROUPS - s, GROUPS)

        def act(rows):
            y_copy(y, s, rows, up_y, g_zs.at[g]).wait_recv()
            y_copy(y, s, rows, up_y, y_l.at[s]).start()
            y_copy(y, s, rows, down_y, y_r.at[s]).start()

        by_size(y, act)

    def y_step(s):
        def left(rows):
            y_copy(down_y, s, rows, up_y, y_l.at[s]).wait_recv()
            if s % 2 == 0:
                y_copy(down_y, s, rows, up_y, y_o.at[s], y_fs.at[s]).start()

        def right(rows):
            y_copy(up_y, s, rows, up_y, y_r.at[s]).wait_recv()
            if s % 2 == 1:
                y_copy(up_y, s, rows, down_y, y_o.at[s], y_fs.at[s]).start()

        by_size(down_y, left)
        by_size(up_y, right)

    def far_step(s):
        by_size(far_y, lambda rows: y_copy(far_y, s, rows, up_y, y_o.at[s]).wait_recv())
        g = lax.rem(grp + GROUPS - s, GROUPS)
        last = spread_b(g_recv[3, slots_of(g)], g_recv[2, slots_of(g), 0:32], tmp)
        o = nn(up[...], tmp[...])
        gj[:, rows_of(g), 256:V] = o.reshape(L, GR, 256)[:, :, 0:192].astype(BF)
        spread_a(g_recv[0, slots_of(g)], g_recv[1, slots_of(g)], tmp)
        o = nn(up[...], tmp[...])
        gj[:, rows_of(g), 0:256] = o.reshape(L, GR, 256).astype(BF)
        fix = nn(ulast[...], last)
        gj[L - 1, rows_of(g), 0:256] = (o[GR * (L - 1) :] + fix).astype(BF)

    for n in range(2, 8):
        loads[n].wait()

    def c_part(c, carry):
        x = gk[c]
        cs[c] = nt(tij[...], x) + nn(x, tij[...])
        return carry

    def a_part(i, carry):
        x = gi[i]
        w[i, :, 0:V] = nt(x, kamp[0, 1]) + nt(tjt[...], x)
        return carry

    lax.fori_loop(0, 3, c_part, 0)
    z_step(0)
    lax.fori_loop(3, 6, c_part, 0)
    z_step(1)
    y_step(0)
    lax.fori_loop(6, L, c_part, 0)
    tjt[...] = kamp[0, 1].astype(F32).T.astype(BF)
    tit[...] = kamp[0, 0].astype(F32).T.astype(BF)
    z_step(2)
    y_step(1)
    xb[:, :, 384:512] = jnp.zeros((L, V, 128), BF)
    vrow[...] = jnp.ones_like(vrow)
    vrow[0:1, 0:V] = vir_ref[...]
    z_step(3)
    y_step(2)
    far_step(0)
    w[:, :, 384:512] = jnp.zeros((L, V, 128), F32)
    lax.fori_loop(0, 2, a_part, 0)
    y_step(3)
    far_step(1)
    far_step(2)
    lax.fori_loop(2, 5, a_part, 0)
    far_step(3)

    def send_a(src, dst, n):
        def step(s, c):
            g = lax.rem(grp + s, GROUPS)
            m0, m1 = packed_a(xb[:, rows_of(g), 0:256].reshape(L * GR, 256), pk)
            src[slots_of(g), 0:48] = m0
            src[slots_of(g), 48:96] = m1
            send_group(src, dst, g, a_ss.at[n], a_rs.at[n])
            return c

        lax.fori_loop(0, GROUPS, step, 0)

    def send_b(src, dst, n):
        def step(s, c):
            g = lax.rem(grp + s, GROUPS)
            x = xb[:, rows_of(g), 256:512].reshape(L * GR, 256)
            m0, mixed = packed_b(x, xb[L - 1, rows_of(g), 0:256], pk, plast)
            src[slots_of(g), 0:48] = m0
            src[slots_of(g), 48:80] = mixed
            send_group(src, dst, g, a_ss.at[n], a_rs.at[n])
            return c

        lax.fori_loop(0, GROUPS, step, 0)

    def all_of(src, dst, n):
        return pltpu.make_async_remote_copy(
            src_ref=src, dst_ref=dst, send_sem=a_ss.at[n], recv_sem=a_rs.at[n],
            device_id={"vir": lax.rem(v + 1, N), "trip": y}, device_id_type=MESH,
        )

    def s_a(c, carry):
        xb[c, :, 0:256] = (cs[c, :, 0:256] + nt(kamp[0, 0], gj[c, 0:256])).astype(BF)
        return carry

    lax.fori_loop(0, L, s_a, 0)
    send_a(sa_send, sa_recv, 0)

    def s_b(c, carry):
        xb[c, :, 256:V] = (cs[c, :, 256:V] + nt(kamp[0, 0], gj[c, 256:V])).astype(BF)
        return carry

    lax.fori_loop(0, L, s_b, 0)
    send_b(sb_send, sb_recv, 1)

    def b_part(i, carry):
        w[i, :, 0:V] = w[i, :, 0:V] + nt(tit[...], gj[i])
        return carry

    lax.fori_loop(5, L, a_part, 0)
    lax.fori_loop(0, L, b_part, 0)

    shift = occ_ref[trip_ref[0, 0]] + occ_ref[trip_ref[0, 1]] + occ_ref[trip_ref[0, 2]]
    vcol = jnp.sum(
        jnp.where(iota((V, V), 0) == iota((V, V), 1), vrow[0:1, 0:V], 0.0), axis=1, keepdims=True
    )

    index = iota((V, 1), 0)
    late = (index - 7 * ((index * 9363) >> 16)) == L - 1

    def weigh(i, lanes, mask, e):
        x = w[i, :, lanes]
        den = vcol + (vrow[0:1, lanes] + (virs_ref[v * L + i] - shift))
        z = x / den
        xb[i, :, lanes] = z.astype(BF)
        t = x * z
        if mask is not None:
            t = jnp.where(mask, t, 0.0)
        return e + jnp.sum(t, axis=0, keepdims=True)

    first, rest = slice(0, 256), slice(256, 512)
    all_of(sa_send, sa_recv, 0).wait_recv()

    def add_a(g, c):
        spread_a(sa_recv[slots_of(g), 0:48], sa_recv[slots_of(g), 48:96], tmp)
        o = nn(up[...], tmp[...]).reshape(L, GR, 256)
        w[:, rows_of(g), first] = w[:, rows_of(g), first] + o
        return c

    lax.fori_loop(0, GROUPS, add_a, 0)
    e = jnp.zeros((1, 256), F32)
    e = lax.fori_loop(0, L - 1, lambda i, e: weigh(i, first, None, e), e)
    e = weigh(L - 1, first, jnp.logical_not(late), e)
    send_a(ya_send, ya_recv, 2)

    def gram_a(i, acc):
        x = xb[i, :, first]
        return acc + nt(x, x)

    cs[0] = lax.fori_loop(0, L - 1, gram_a, jnp.zeros((V, V), F32))

    all_of(sb_send, sb_recv, 1).wait_recv()

    def add_b(g, c):
        last = spread_b(sb_recv[slots_of(g), 0:48], sb_recv[slots_of(g), 48:80], tmp)
        o = nn(up[...], tmp[...]).reshape(L, GR, 256)
        w[:, rows_of(g), rest] = w[:, rows_of(g), rest] + o
        w[L - 1, rows_of(g), first] = w[L - 1, rows_of(g), first] + nn(ulast[...], last)
        return c

    lax.fori_loop(0, GROUPS, add_b, 0)
    e = lax.fori_loop(0, L, lambda i, e: weigh(i, rest, None, e), e)
    e = weigh(L - 1, first, late, e)
    send_b(yb_send, yb_recv, 3)

    def gram_b(i, acc):
        x = xb[i, :, rest]
        return acc + nt(x, x)

    x = xb[L - 1, :, first]
    total = lax.fori_loop(0, L, gram_b, cs[0] + nt(x, x))

    hi = total.astype(BF)
    left = total - hi.astype(F32)
    mid = left.astype(BF)
    lo = (left - mid.astype(F32)).astype(BF)
    rows = nn(rowm[...], hi) + nn(rowm[...], mid) + nn(rowm[...], lo)
    energy = jnp.sum(e)
    gram[:, 384:512] = jnp.zeros((N * 8, 128), F32)
    gram[:, 0:V] = rows
    spare = lax.rem(iota((N * 8, 128), 0), 8) == 7
    mine = spare & (iota((N * 8, 128), 1) == y)
    gram[:, 0:128] = jnp.where(mine, energy, gram[:, 0:128])

    piece = y * 2 + core

    def piece_copy(k):
        to = lax.rem(piece + k, 8)
        return pltpu.make_async_remote_copy(
            src_ref=gram.at[pl.ds(pl.multiple_of(to * 64, 64), 64)], dst_ref=d1.at[piece],
            send_sem=d1_ss, recv_sem=d1_rs,
            device_id={"vir": chip * 2 + lax.rem(to, 2), "trip": to // 2}, device_id_type=MESH,
        )

    for k in range(1, 8):
        piece_copy(k).start()
    pltpu.make_async_copy(
        gram.at[pl.ds(pl.multiple_of(piece * 64, 64), 64)], d1.at[piece], d1_rs
    ).start()

    all_of(ya_send, ya_recv, 2).wait_recv()

    def take_a(g, c):
        spread_a(ya_recv[slots_of(g), 0:48], ya_recv[slots_of(g), 48:96], tmp)
        o = nn(up[...], tmp[...]).reshape(L, GR, 256)
        gk[:, rows_of(g), 0:256] = o.astype(BF)
        return c

    lax.fori_loop(0, GROUPS, take_a, 0)

    def out_first(c, carry):
        x = gk[c, :, 0:256]
        cs[c] = nt(x, tij[:, 0:256])
        cs[c, 0:256] = cs[c, 0:256] + tn(x, tij[...])
        return carry

    lax.fori_loop(0, L - 1, out_first, 0)

    pltpu.make_async_copy(d1, d1, d1_rs).wait()
    d2s[...] = jnp.sum(d1[...], axis=0)

    def owner_send(o, c):
        to = piece * 8 + o
        src = d2s.at[pl.ds(pl.multiple_of(o * 8, 8), 8)]

        @pl.when(to != v)
        def _():
            pltpu.make_async_remote_copy(
                src_ref=src, dst_ref=d2.at[chip], send_sem=d2_ss, recv_sem=d2_rs,
                device_id={"vir": to, "trip": y}, device_id_type=MESH,
            ).start()

        @pl.when(to == v)
        def _():
            pltpu.make_async_copy(src, d2.at[chip], d2_rs).start()

        return c

    lax.fori_loop(0, 8, owner_send, 0)

    is_owner = y == grp

    def fin_copy(ty):
        return pltpu.make_async_remote_copy(
            src_ref=dfin, dst_ref=dfin, send_sem=d3_ss, recv_sem=d3_rs,
            device_id={"vir": v, "trip": ty}, device_id_type=MESH,
        )

    all_of(yb_send, yb_recv, 3).wait_recv()

    def take_b(g, c):
        last = spread_b(yb_recv[slots_of(g), 0:48], yb_recv[slots_of(g), 48:80], tmp)
        o = nn(up[...], tmp[...]).reshape(L, GR, 256)
        gk[:, rows_of(g), 256:V] = o[:, :, 0:192].astype(BF)
        fix = gk[L - 1, rows_of(g), first].astype(F32) + nn(ulast[...], last)
        gk[L - 1, rows_of(g), first] = fix.astype(BF)
        return c

    lax.fori_loop(0, GROUPS, take_b, 0)

    @pl.when(is_owner)
    def _():
        pltpu.make_async_copy(d2, d2, d2_rs).wait()
        dfin[...] = jnp.sum(d2[...], axis=0)
        for dy in (1, 2, 3):
            fin_copy(lax.rem(y + dy, 4)).start()

    def out_last(c, carry):
        x = gk[c, :, 256:V]
        acc = cs[c] + nt(x, tij[:, 256:V])
        gi[c, 0:256] = acc[0:256].astype(BF)
        gi[c, 256:V] = (acc[256:V] + tn(x, tij[...])).astype(BF)
        pltpu.make_async_copy(gi.at[c], vvvo_hbm.at[0, c], ld.at[0]).start()
        return carry

    x = gk[L - 1]
    gi[L - 1] = (nt(x, tij[...]) + tn(x, tij[...])).astype(BF)
    pltpu.make_async_copy(gi.at[L - 1], vvvo_hbm.at[0, L - 1], ld.at[0]).start()
    lax.fori_loop(0, L - 1, out_last, 0)

    @pl.when(jnp.logical_not(is_owner))
    def _():
        fin_copy(y).wait_recv()

    density_ref[...] = dfin[0:7, 0:V] * (1.0 / (V * V))
    sel = iota((1, 128), 1) == y
    es = jnp.sum(jnp.where(sel, dfin[7:8, 0:128], 0.0), axis=1, keepdims=True)
    energy_ref[...] = jnp.broadcast_to(es * (1.0 / V**3), (8, 128))

    pltpu.make_async_copy(gi, vvvo_hbm.at[0], ld.at[0]).wait()
    def drain_g(rows):
        part = g_send.at[0, pl.ds(0, N - 1), pl.ds(0, rows)]
        pltpu.make_async_remote_copy(
            src_ref=part, dst_ref=part, send_sem=g_ss, recv_sem=g_ss,
            device_id={"vir": v, "trip": up_y}, device_id_type=MESH,
        ).wait_send()

    by_size(y, drain_g)
    for s in range(GROUPS):

        def drain_y(rows):
            part = g_send.at[0, pl.ds(0, 2 * GD), pl.ds(0, rows)]
            pltpu.make_async_remote_copy(
                src_ref=part, dst_ref=part, send_sem=y_ss.at[s], recv_sem=g_ss,
                device_id={"vir": v, "trip": up_y}, device_id_type=MESH,
            ).wait_send()

        by_size(y, drain_y)
        by_size(
            down_y if s % 2 == 0 else up_y,
            lambda rows: y_copy(y, s, rows, up_y, g_ss, y_fs.at[s]).wait_send(),
        )
    for n, buf in enumerate((sa_send, sb_send, ya_send, yb_send)):
        part = buf.at[pl.ds(0, N - 1)]
        all_of(part, part, n).wait_send()
    part = d1.at[pl.ds(0, 7)]
    pltpu.make_async_remote_copy(
        src_ref=part, dst_ref=part, send_sem=d1_ss, recv_sem=d1_ss,
        device_id={"vir": v, "trip": up_y}, device_id_type=MESH,
    ).wait_send()

    def drain_owner(count):
        q = d2.at[pl.ds(0, count)]
        pltpu.make_async_remote_copy(
            src_ref=q, dst_ref=q, send_sem=d2_ss, recv_sem=d2_ss,
            device_id={"vir": v, "trip": up_y}, device_id_type=MESH,
        ).wait_send()

    own_piece = (v // 8) == piece

    @pl.when(own_piece)
    def _():
        drain_owner(7)

    @pl.when(jnp.logical_not(own_piece))
    def _():
        drain_owner(8)

    @pl.when(is_owner)
    def _():
        for dy in (1, 2, 3):
            fin_copy(lax.rem(y + dy, 4)).wait_send()


def body(triplets, pair_integrals, k_integrals, pair_amplitudes, k_amplitudes, occ_energy, vir_energy):
    vm = pl.BlockSpec(memory_space=pltpu.VMEM)
    sm = pl.BlockSpec(memory_space=pltpu.SMEM)
    hbm = pl.BlockSpec(memory_space=pl.ANY)
    slab = pltpu.VMEM((L, V, V), BF)
    dma = pltpu.SemaphoreType.DMA
    energy, density, vvvo = pl.pallas_call(
        kernel,
        out_shape=(
            jax.ShapeDtypeStruct((8, 128), F32),
            jax.ShapeDtypeStruct((L, V), F32),
            jax.ShapeDtypeStruct((1, L, V, V), BF),
        ),
        in_specs=[sm, sm, sm, vm, hbm, hbm, hbm, hbm, hbm, hbm, hbm, vm, vm],
        out_specs=(vm, vm, hbm),
        scratch_shapes=[
            slab, slab, slab,
            pltpu.VMEM((V, V), BF),
            pltpu.VMEM((1, 2, V, V), BF),
            pltpu.VMEM((GD * SLOT, L * GR), BF),
            pltpu.VMEM((L * GR, GD * SLOT), BF),
            pltpu.VMEM((N * 8, V), BF),
            pltpu.VMEM((L, V, V), F32),
            pltpu.VMEM((L, V, 512), F32),
            pltpu.VMEM((L, V, 512), BF),
            pltpu.VMEM((V, V), BF),
            pltpu.VMEM((V, V), BF),
            pltpu.VMEM((8, 512), F32),
            pltpu.VMEM((GD * SLOT, 256), BF),
            pltpu.VMEM((4, N, 48, 128), BF),
            pltpu.VMEM((4, N, 48, 128), BF),
            pltpu.VMEM((N, ROWS_A, 128), BF),
            pltpu.VMEM((N, ROWS_A, 128), BF),
            pltpu.VMEM((N, ROWS_B, 128), BF),
            pltpu.VMEM((N, ROWS_B, 128), BF),
            pltpu.VMEM((N, ROWS_A, 128), BF),
            pltpu.VMEM((N, ROWS_A, 128), BF),
            pltpu.VMEM((N, ROWS_B, 128), BF),
            pltpu.VMEM((N, ROWS_B, 128), BF),
            pltpu.VMEM((N * 8, 512), F32),
            pltpu.VMEM((8, 64, 512), F32),
            pltpu.VMEM((32, 8, 512), F32),
            pltpu.VMEM((64, 512), F32),
            pltpu.VMEM((8, 512), F32),
            dma((8,)), dma, dma((4,)), dma((4,)), dma((4,)), dma((4,)), dma((4,)), dma((4,)),
            dma((4,)), dma((4,)), dma, dma, dma, dma, dma, dma,
        ],
        compiler_params=pltpu.CompilerParams(
            collective_id=0, has_side_effects=True, vmem_limit_bytes=60 * 1024 * 1024
        ),
        name="triples",
    )(
        triplets, occ_energy, vir_energy, vir_energy.reshape(1, V), pair_integrals, k_integrals,
        pair_amplitudes, k_amplitudes,
        jnp.asarray(pack_matrix(), BF), jnp.asarray(unpack_matrix(), BF), jnp.asarray(row_matrix(), BF),
        jnp.asarray(pack_last(), BF), jnp.asarray(unpack_last(), BF),
    )
    return energy[0, 0:1], density, vvvo


def solution(mesh):
    return jax.shard_map(
        body,
        mesh=mesh,
        in_specs=(
            P("trip", None),
            P(None, "vir", None, None),
            P("trip", "vir", None, None),
            P(),
            P("trip", None, None, None),
            P(),
            P(),
        ),
        out_specs=(P("trip"), P("vir", None), P("trip", "vir", None, None)),
        check_vma=False,
    )
```

time: 227 us -> 199 us (0.88)
  Pallas kernels: 220 us -> 190 us
    pallas_call x1, Pallas kernels: 220 us -> 190 us  [body(): pl.pallas_call(kernel, out_shape=(jax.ShapeDtypeStruct((8, 128), F32), ja...]
where the time goes in v2:
time: 199 us; the launch traced here: 197 us
  Pallas kernels  190 us (95%)
  local copies, waits for them, and re-layouts  6.41 us (3%)
    pallas_call x1, Pallas kernels, body(): pl.pallas_call(kernel, out_shape=(jax.ShapeDtypeStruct((8, 128), F32), ja...  190 us
    unnamed x2, local copies, waits for them, and re-layouts  5.22 us

profile of v2, /device:TPU:1, one launch (start us, length us, event | category | flops | bytes accessed | tf_op | source)
XLA Modules:
  0.0 196.8 jit_solution(8321185717433122880)
XLA Ops:
  0.6 189.8 %triples.1 = (f32[8,128]{1,0:T(8,128)}, f32[7,448]{1,0:T(8,128)}, bf16[1,7,448,448]{3,2,1,0:T(8,128)(2,1)}) custom-call(s32[1,3]{1,0:T(1,128)} %trip_ref.1, f32[120]{0:T(128)} %occ_ref.1, f32[448]{0:T(512)} %virs_ref.1, f32[1,448]{1,0:T(1,128)} %bitcast.2, bf16[2,7,448,448]{3,2,1,0:T(8,128)(2,1)} %pair_hbm.1, bf16[1,7,448,448]{3,2,1,0:T(8,128)(2,1)} %k_hbm.1, ...), custom_call_target="tpu_custom_call" | custom-call | tf_op jit(solution)/shard_map/triples/pallas_call | solution.py:609
  190.4 1.2 slice.3
  191.6 1.3 copy.17
  192.9 3.9 %copy.18 = bf16[1,7,448,448]{3,2,1,0:T(8,128)(2,1)} copy(bf16[1,7,448,448]{3,2,1,0:T(8,128)(2,1)} %get-tuple-element.14) | data formatting | bytes 5619712

commit v3 on v2

--- a/solution.py
+++ b/solution.py
@@ -48,6 +48,24 @@
     for j in range(GD):
         m[j, L - 1, j, 0] = 1
     return m.reshape(GR, GD * 8)
+
+
+def turn_pack_matrix():
+    m = np.zeros((GD, 32, 4, GD, L), np.float32)
+    for p in range(4):
+        for q in range(L):
+            for j in range(GD):
+                m[j, L * p + q, p, j, q] = 1
+    return m.reshape(GD * 32, 4 * GR)
+
+
+def turn_unpack_matrix():
+    m = np.zeros((L, 4, GD, GD, 32), np.float32)
+    for p in range(4):
+        for q in range(L):
+            for k in range(GD):
+                m[q, p, k, k, L * p + q] = 1
+    return m.reshape(L * 4 * GD, GD * 32)
 
 
 def row_matrix():
@@ -122,9 +140,9 @@
 
 
 def kernel(
-    trip_ref, occ_ref, virs_ref, vir_ref, pair_hbm, k_hbm, tij_hbm, kamp_hbm, pk_hbm, up_hbm, row_hbm, plast, ulast,
+    trip_ref, occ_ref, virs_ref, vir_ref, pair_hbm, k_hbm, tij_hbm, kamp_hbm, pk_hbm, up_hbm, row_hbm, plast, ulast, pkt, upt,
     energy_ref, density_ref, vvvo_hbm,
-    gi, gj, gk, tij, kamp, pk, up, rowm, cs, w, xb, tjt, tit, vrow, tmp,
+    gi, gj, gk, tij, kamp, pk, up, rowm, cs, w, xb, tjt, tit, tjp, tijp, pm, pmt, vrow, tmp, tmpt,
     g_send, g_recv, sa_send, sa_recv, sb_send, sb_recv, ya_send, ya_recv, yb_send, yb_recv,
     gram, d1, d2, d2s, dfin,
     ld, g_ss, g_zs, y_ss, y_fs, y_l, y_r, y_o, a_ss, a_rs, d1_ss, d1_rs, d2_ss, d2_rs, d3_ss, d3_rs,
@@ -140,13 +158,12 @@
         pltpu.make_async_copy(src, dst, ld.at[n])
         for n, (src, dst) in enumerate(
             (
-                (pk_hbm, pk), (pair_hbm.at[1], gj), (k_hbm.at[0], gk), (tij_hbm, tij),
+                (pair_hbm.at[1], gj), (k_hbm.at[0], gk), (tij_hbm, tij), (pk_hbm, pk),
                 (pair_hbm.at[0], gi), (kamp_hbm, kamp), (up_hbm, up), (row_hbm, rowm),
             )
         )
     ]
-    for n in range(2):
-        loads[n].start()
+    loads[0].start()
 
     barrier = pltpu.get_barrier_semaphore()
 
@@ -165,10 +182,10 @@
             barrier, inc=1, device_id={"vir": partner, "trip": ty}, device_id_type=MESH
         )
 
-    for n in range(2):
-        loads[n].wait()
-    for n in range(2, 8):
+    loads[0].wait()
+    for n in range(1, 8):
         loads[n].start()
+    xb[:, :, 384:512] = jnp.zeros((L, V, 128), BF)
 
     def send_group(src, dst, g, ss, rs):
         def one(k, c):
@@ -195,128 +212,111 @@
     def slots_of(g):
         return pl.ds(g * GD, GD)
 
+    tile = pl.ds(pl.multiple_of(y * 128, 128), 128)
+
     def turn(s, c):
         g = lax.rem(grp + s, GROUPS)
-        x = gj[:, rows_of(g), 0:256].reshape(L * GR, 256)
-        m0, m1 = packed_a(x, pk)
-        g_send[0, slots_of(g)] = m0
-        g_send[1, slots_of(g)] = m1
-        z = jnp.concatenate([gj[:, rows_of(g), 256:V], jnp.zeros((L, GR, 64), BF)], axis=2)
-        m0, mixed = packed_b(z.reshape(L * GR, 256), gj[L - 1, rows_of(g), 0:256], pk, plast)
-        g_send[3, slots_of(g)] = m0
-        g_send[2, slots_of(g), 0:32] = mixed
+        xb[:, rows_of(g), 0:V] = gj[:, rows_of(g), :]
+        x = xb[0:4, rows_of(g), tile].reshape(4 * GR, 128)
+        g_send[0, slots_of(g)] = nn(pkt[...], x).astype(BF).reshape(GD, 32, 128)
 
         @pl.when(s == 0)
         def _():
             pl.semaphore_wait(barrier, N - 1 + 6)
 
-        @pl.when(y != 2)
-        def _():
-            send_group(g_send.at[y], g_recv.at[y], g, g_ss, g_zs.at[grp])
-
-        @pl.when(y == 2)
-        def _():
-            send_group(
-                g_send.at[2, :, pl.ds(0, 32)], g_recv.at[2, :, pl.ds(0, 32)], g, g_ss, g_zs.at[grp]
-            )
-
+        send_group(g_send.at[0], g_recv.at[0, y], g, g_ss.at[0], g_zs.at[grp])
+        return c
+
+    def turn_rest(s, c):
+        g = lax.rem(grp + s, GROUPS)
+        x = xb[4:L, rows_of(g), tile].reshape(3 * GR, 128)
+        g_send[1, slots_of(g)] = nn(pkt[:, 0 : 3 * GR], x).astype(BF).reshape(GD, 32, 128)
+        send_group(g_send.at[1], g_recv.at[1, y], g, g_ss.at[1], g_zs.at[GROUPS + grp])
         return c
 
     lax.fori_loop(0, GROUPS, turn, 0)
+    lax.fori_loop(0, GROUPS, turn_rest, 0)
 
     up_y, down_y = lax.rem(y + 1, 4), lax.rem(y + 3, 4)
     far_y = lax.rem(y + 2, 4)
 
-    def by_size(q, act):
-        @pl.when(q != 2)
-        def _():
-            act(48)
-
-        @pl.when(q == 2)
-        def _():
-            act(32)
-
-    def y_copy(q, s, rows, ty, rs, ss=None):
-        g = lax.rem(grp + GROUPS - s, GROUPS)
-        piece = g_recv.at[q, slots_of(g), pl.ds(0, rows)]
+    def group_at(s):
+        return lax.rem(grp + GROUPS - s, GROUPS)
+
+    def y_copy(h, q, s, ty, rs, ss):
+        piece = g_recv.at[h, q, slots_of(group_at(s))]
         return pltpu.make_async_remote_copy(
-            src_ref=piece, dst_ref=piece,
-            send_sem=y_ss.at[s] if ss is None else ss, recv_sem=rs,
-            device_id={"vir": v, "trip": ty}, device_id_type=MESH,
-        )
-
-    def z_step(s):
-        g = lax.rem(grp + GROUPS - s, GROUPS)
-
-        def act(rows):
-            y_copy(y, s, rows, up_y, g_zs.at[g]).wait_recv()
-            y_copy(y, s, rows, up_y, y_l.at[s]).start()
-            y_copy(y, s, rows, down_y, y_r.at[s]).start()
-
-        by_size(y, act)
-
-    def y_step(s):
-        def left(rows):
-            y_copy(down_y, s, rows, up_y, y_l.at[s]).wait_recv()
-            if s % 2 == 0:
-                y_copy(down_y, s, rows, up_y, y_o.at[s], y_fs.at[s]).start()
-
-        def right(rows):
-            y_copy(up_y, s, rows, up_y, y_r.at[s]).wait_recv()
-            if s % 2 == 1:
-                y_copy(up_y, s, rows, down_y, y_o.at[s], y_fs.at[s]).start()
-
-        by_size(down_y, left)
-        by_size(up_y, right)
-
-    def far_step(s):
-        by_size(far_y, lambda rows: y_copy(far_y, s, rows, up_y, y_o.at[s]).wait_recv())
-        g = lax.rem(grp + GROUPS - s, GROUPS)
-        last = spread_b(g_recv[3, slots_of(g)], g_recv[2, slots_of(g), 0:32], tmp)
-        o = nn(up[...], tmp[...])
-        gj[:, rows_of(g), 256:V] = o.reshape(L, GR, 256)[:, :, 0:192].astype(BF)
-        spread_a(g_recv[0, slots_of(g)], g_recv[1, slots_of(g)], tmp)
-        o = nn(up[...], tmp[...])
-        gj[:, rows_of(g), 0:256] = o.reshape(L, GR, 256).astype(BF)
-        fix = nn(ulast[...], last)
-        gj[L - 1, rows_of(g), 0:256] = (o[GR * (L - 1) :] + fix).astype(BF)
-
-    for n in range(2, 8):
+            src_ref=piece, dst_ref=piece, send_sem=ss.at[GROUPS * h + s],
+            recv_sem=rs, device_id={"vir": v, "trip": ty}, device_id_type=MESH,
+        )
+
+    def z_step(h, s):
+        y_copy(h, y, s, up_y, g_zs.at[GROUPS * h + group_at(s)], y_ss).wait_recv()
+        y_copy(h, y, s, up_y, y_l.at[GROUPS * h + s], y_ss).start()
+        y_copy(h, y, s, down_y, y_r.at[GROUPS * h + s], y_ss).start()
+
+    def y_step(h, s):
+        n = GROUPS * h + s
+        y_copy(h, down_y, s, up_y, y_l.at[n], y_ss).wait_recv()
+        if s % 2 == 0:
+            y_copy(h, down_y, s, up_y, y_o.at[n], y_fs).start()
+        y_copy(h, up_y, s, up_y, y_r.at[n], y_ss).wait_recv()
+        if s % 2 == 1:
+            y_copy(h, up_y, s, down_y, y_o.at[n], y_fs).start()
+
+    def far_step(h, s):
+        y_copy(h, far_y, s, up_y, y_o.at[GROUPS * h + s], y_ss).wait_recv()
+        g = group_at(s)
+        for t in range(4):
+            tmpt[:, 128 * t : 128 * t + 128] = g_recv[h, t, slots_of(g)].reshape(GD * 32, 128)
+        o = nn(upt[...], tmpt[...]).astype(BF)
+        for q in range(L):
+            for p in range(4 - h):
+                at = pl.ds(pl.multiple_of(64 * (4 * h + p) + GD * g, GD), GD)
+                gj[q, at, :] = o[GD * (4 * q + p) : GD * (4 * q + p + 1), 0:V]
+
+    pm[...] = jnp.where(
+        iota((V, V), 1) == 7 * (iota((V, V), 0) & 63) + (iota((V, V), 0) >> 6), 1.0, 0.0
+    ).astype(BF)
+    pmt[...] = jnp.where(
+        iota((V, V), 0) == 7 * (iota((V, V), 1) & 63) + (iota((V, V), 1) >> 6), 1.0, 0.0
+    ).astype(BF)
+    for n in range(1, 3):
         loads[n].wait()
+    tijp[...] = nt(tij[...], pm[...]).astype(BF)
 
     def c_part(c, carry):
         x = gk[c]
-        cs[c] = nt(tij[...], x) + nn(x, tij[...])
+        cs[c] = nt(tij[...], nn(pm[...], x).astype(BF)) + nn(x, tijp[...])
         return carry
 
     def a_part(i, carry):
         x = gi[i]
-        w[i, :, 0:V] = nt(x, kamp[0, 1]) + nt(tjt[...], x)
+        w[i, :, 0:V] = nt(x, tjp[...]) + nt(tjt[...], nn(pm[...], x).astype(BF))
         return carry
 
     lax.fori_loop(0, 3, c_part, 0)
-    z_step(0)
+    z_step(0, 0)
     lax.fori_loop(3, 6, c_part, 0)
-    z_step(1)
-    y_step(0)
+    z_step(0, 1)
+    y_step(0, 0)
     lax.fori_loop(6, L, c_part, 0)
-    tjt[...] = kamp[0, 1].astype(F32).T.astype(BF)
-    tit[...] = kamp[0, 0].astype(F32).T.astype(BF)
-    z_step(2)
-    y_step(1)
-    xb[:, :, 384:512] = jnp.zeros((L, V, 128), BF)
-    vrow[...] = jnp.ones_like(vrow)
-    vrow[0:1, 0:V] = vir_ref[...]
-    z_step(3)
-    y_step(2)
-    far_step(0)
-    w[:, :, 384:512] = jnp.zeros((L, V, 128), F32)
-    lax.fori_loop(0, 2, a_part, 0)
-    y_step(3)
-    far_step(1)
-    far_step(2)
-    lax.fori_loop(2, 5, a_part, 0)
-    far_step(3)
+    for n in range(3, 8):
+        loads[n].wait()
+    z_step(0, 2)
+    y_step(0, 1)
+    z_step(0, 3)
+    y_step(0, 2)
+    z_step(1, 0)
+    far_step(0, 0)
+    y_step(0, 3)
+    z_step(1, 1)
+    far_step(0, 1)
+    far_step(0, 2)
+    z_step(1, 2)
+    far_step(0, 3)
+    z_step(1, 3)
+    y_step(1, 0)
 
     def send_a(src, dst, n):
         def step(s, c):
@@ -354,6 +354,26 @@
     lax.fori_loop(0, L, s_a, 0)
     send_a(sa_send, sa_recv, 0)
 
+    y_step(1, 1)
+    tjt[...] = kamp[0, 1].astype(F32).T.astype(BF)
+    tit[...] = kamp[0, 0].astype(F32).T.astype(BF)
+    tjp[...] = nn(pm[...], kamp[0, 1]).astype(BF)
+    vrow[...] = jnp.ones_like(vrow)
+    vcol = jnp.sum(
+        jnp.where(iota((V, V), 0) == iota((V, V), 1), vir_ref[...], 0.0), axis=1, keepdims=True
+    )
+    vrow[0:1, 0:V] = jnp.sum(
+        jnp.where(iota((V, V), 0) == 7 * (iota((V, V), 1) & 63) + (iota((V, V), 1) >> 6), vcol, 0.0),
+        axis=0, keepdims=True,
+    )
+    y_step(1, 2)
+    far_step(1, 0)
+    y_step(1, 3)
+    far_step(1, 1)
+    far_step(1, 2)
+    far_step(1, 3)
+    w[:, :, 384:512] = jnp.zeros((L, V, 128), F32)
+
     def s_b(c, carry):
         xb[c, :, 256:V] = (cs[c, :, 256:V] + nt(kamp[0, 0], gj[c, 256:V])).astype(BF)
         return carry
@@ -365,14 +385,10 @@
         w[i, :, 0:V] = w[i, :, 0:V] + nt(tit[...], gj[i])
         return carry
 
-    lax.fori_loop(5, L, a_part, 0)
+    lax.fori_loop(0, L, a_part, 0)
     lax.fori_loop(0, L, b_part, 0)
 
     shift = occ_ref[trip_ref[0, 0]] + occ_ref[trip_ref[0, 1]] + occ_ref[trip_ref[0, 2]]
-    vcol = jnp.sum(
-        jnp.where(iota((V, V), 0) == iota((V, V), 1), vrow[0:1, 0:V], 0.0), axis=1, keepdims=True
-    )
-
     index = iota((V, 1), 0)
     late = (index - 7 * ((index * 9363) >> 16)) == L - 1
 
@@ -468,8 +484,10 @@
 
     def out_first(c, carry):
         x = gk[c, :, 0:256]
-        cs[c] = nt(x, tij[:, 0:256])
-        cs[c, 0:256] = cs[c, 0:256] + tn(x, tij[...])
+        r = tn(x, tij[...])
+        top = r.astype(BF)
+        low = (r - top.astype(F32)).astype(BF)
+        cs[c] = nt(x, tijp[:, 0:256]) + (nn(pmt[:, 0:256], top) + nn(pmt[:, 0:256], low))
         return carry
 
     lax.fori_loop(0, L - 1, out_first, 0)
@@ -525,14 +543,14 @@
 
     def out_last(c, carry):
         x = gk[c, :, 256:V]
-        acc = cs[c] + nt(x, tij[:, 256:V])
-        gi[c, 0:256] = acc[0:256].astype(BF)
-        gi[c, 256:V] = (acc[256:V] + tn(x, tij[...])).astype(BF)
+        r = tn(x, tij[...]).astype(BF)
+        gi[c] = (cs[c] + (nt(x, tijp[:, 256:V]) + nn(pmt[:, 256:V], r))).astype(BF)
         pltpu.make_async_copy(gi.at[c], vvvo_hbm.at[0, c], ld.at[0]).start()
         return carry
 
     x = gk[L - 1]
-    gi[L - 1] = (nt(x, tij[...]) + tn(x, tij[...])).astype(BF)
+    r = tn(x, tij[...]).astype(BF)
+    gi[L - 1] = (nt(x, tijp[...]) + nn(pmt[...], r)).astype(BF)
     pltpu.make_async_copy(gi.at[L - 1], vvvo_hbm.at[0, L - 1], ld.at[0]).start()
     lax.fori_loop(0, L - 1, out_last, 0)
 
@@ -546,28 +564,19 @@
     energy_ref[...] = jnp.broadcast_to(es * (1.0 / V**3), (8, 128))
 
     pltpu.make_async_copy(gi, vvvo_hbm.at[0], ld.at[0]).wait()
-    def drain_g(rows):
-        part = g_send.at[0, pl.ds(0, N - 1), pl.ds(0, rows)]
+    for h in range(2):
+        part = g_send.at[0, pl.ds(0, N - 1)]
         pltpu.make_async_remote_copy(
-            src_ref=part, dst_ref=part, send_sem=g_ss, recv_sem=g_ss,
+            src_ref=part, dst_ref=part, send_sem=g_ss.at[h], recv_sem=y_l.at[0],
             device_id={"vir": v, "trip": up_y}, device_id_type=MESH,
         ).wait_send()
-
-    by_size(y, drain_g)
-    for s in range(GROUPS):
-
-        def drain_y(rows):
-            part = g_send.at[0, pl.ds(0, 2 * GD), pl.ds(0, rows)]
+        for s in range(GROUPS):
+            part = g_send.at[0, pl.ds(0, 2 * GD)]
             pltpu.make_async_remote_copy(
-                src_ref=part, dst_ref=part, send_sem=y_ss.at[s], recv_sem=g_ss,
+                src_ref=part, dst_ref=part, send_sem=y_ss.at[GROUPS * h + s], recv_sem=y_l.at[0],
                 device_id={"vir": v, "trip": up_y}, device_id_type=MESH,
             ).wait_send()
-
-        by_size(y, drain_y)
-        by_size(
-            down_y if s % 2 == 0 else up_y,
-            lambda rows: y_copy(y, s, rows, up_y, g_ss, y_fs.at[s]).wait_send(),
-        )
+            y_copy(h, y, s, up_y, y_l.at[0], y_fs).wait_send()
     for n, buf in enumerate((sa_send, sb_send, ya_send, yb_send)):
         part = buf.at[pl.ds(0, N - 1)]
         all_of(part, part, n).wait_send()
@@ -613,7 +622,7 @@
             jax.ShapeDtypeStruct((L, V), F32),
             jax.ShapeDtypeStruct((1, L, V, V), BF),
         ),
-        in_specs=[sm, sm, sm, vm, hbm, hbm, hbm, hbm, hbm, hbm, hbm, vm, vm],
+        in_specs=[sm, sm, sm, vm] + [hbm] * 7 + [vm] * 4,
         out_specs=(vm, vm, hbm),
         scratch_shapes=[
             slab, slab, slab,
@@ -625,12 +634,14 @@
             pltpu.VMEM((L, V, V), F32),
             pltpu.VMEM((L, V, 512), F32),
             pltpu.VMEM((L, V, 512), BF),
-            pltpu.VMEM((V, V), BF),
-            pltpu.VMEM((V, V), BF),
+        ]
+        + [pltpu.VMEM((V, V), BF)] * 6
+        + [
             pltpu.VMEM((8, 512), F32),
             pltpu.VMEM((GD * SLOT, 256), BF),
-            pltpu.VMEM((4, N, 48, 128), BF),
-            pltpu.VMEM((4, N, 48, 128), BF),
+            pltpu.VMEM((GD * 32, 512), BF),
+            pltpu.VMEM((2, N, 32, 128), BF),
+            pltpu.VMEM((2, 4, N, 32, 128), BF),
             pltpu.VMEM((N, ROWS_A, 128), BF),
             pltpu.VMEM((N, ROWS_A, 128), BF),
             pltpu.VMEM((N, ROWS_B, 128), BF),
@@ -644,7 +655,7 @@
             pltpu.VMEM((32, 8, 512), F32),
             pltpu.VMEM((64, 512), F32),
             pltpu.VMEM((8, 512), F32),
-            dma((8,)), dma, dma((4,)), dma((4,)), dma((4,)), dma((4,)), dma((4,)), dma((4,)),
+            dma((8,)), dma((2,)), dma((8,)), dma((8,)), dma((8,)), dma((8,)), dma((8,)), dma((8,)),
             dma((4,)), dma((4,)), dma, dma, dma, dma, dma, dma,
         ],
         compiler_params=pltpu.CompilerParams(
@@ -656,6 +667,7 @@
         pair_amplitudes, k_amplitudes,
         jnp.asarray(pack_matrix(), BF), jnp.asarray(unpack_matrix(), BF), jnp.asarray(row_matrix(), BF),
         jnp.asarray(pack_last(), BF), jnp.asarray(unpack_last(), BF),
+        jnp.asarray(turn_pack_matrix(), BF), jnp.asarray(turn_unpack_matrix(), BF),
     )
     return energy[0, 0:1], density, vvvo
 

time: 199 us -> 192 us (0.965); the launches traced: 197 us -> 192 us
  Pallas kernels: 190 us -> 185 us
    pallas_call x1, Pallas kernels: 190 us -> 185 us  [body(): pl.pallas_call(kernel, out_shape=(jax.ShapeDtypeStruct((8, 128), F32), ja...]
where the time goes in v3:
time: 192 us
  Pallas kernels  185 us (96%)
  local copies, waits for them, and re-layouts  6.41 us (3%)
    pallas_call x1, Pallas kernels, body(): pl.pallas_call(kernel, out_shape=(jax.ShapeDtypeStruct((8, 128), F32), ja...  185 us
    unnamed x2, local copies, waits for them, and re-layouts  5.22 us

profile of v3, /device:TPU:1, one launch (start us, length us, event | category | flops | bytes accessed | tf_op | source)
XLA Modules:
  0.0 191.9 jit_solution(9057984127934430911)
XLA Ops:
  0.6 184.9 %triples.1 = (f32[8,128]{1,0:T(8,128)}, f32[7,448]{1,0:T(8,128)}, bf16[1,7,448,448]{3,2,1,0:T(8,128)(2,1)}) custom-call(s32[1,3]{1,0:T(1,128)} %trip_ref.1, f32[120]{0:T(128)} %occ_ref.1, f32[448]{0:T(512)} %virs_ref.1, f32[1,448]{1,0:T(1,128)} %bitcast.2, bf16[2,7,448,448]{3,2,1,0:T(8,128)(2,1)} %pair_hbm.1, bf16[1,7,448,448]{3,2,1,0:T(8,128)(2,1)} %k_hbm.1, ...), custom_call_target="tpu_custom_call" | custom-call | tf_op jit(solution)/shard_map/triples/pallas_call | solution.py:618
  185.5 1.2 slice.3
  186.7 1.3 copy.19
  188.0 3.9 %copy.20 = bf16[1,7,448,448]{3,2,1,0:T(8,128)(2,1)} copy(bf16[1,7,448,448]{3,2,1,0:T(8,128)(2,1)} %get-tuple-element.14) | data formatting | bytes 5619712

commit v4 on v3

--- a/solution.py
+++ b/solution.py
@@ -141,11 +141,11 @@
 
 def kernel(
     trip_ref, occ_ref, virs_ref, vir_ref, pair_hbm, k_hbm, tij_hbm, kamp_hbm, pk_hbm, up_hbm, row_hbm, plast, ulast, pkt, upt,
-    energy_ref, density_ref, vvvo_hbm,
+    small, cs_hbm, xo_hbm, dx_hbm, tijp_hbm, pmt_hbm,
     gi, gj, gk, tij, kamp, pk, up, rowm, cs, w, xb, tjt, tit, tjp, tijp, pm, pmt, vrow, tmp, tmpt,
     g_send, g_recv, sa_send, sa_recv, sb_send, sb_recv, ya_send, ya_recv, yb_send, yb_recv,
     gram, d1, d2, d2s, dfin,
-    ld, g_ss, g_zs, y_ss, y_fs, y_l, y_r, y_o, a_ss, a_rs, d1_ss, d1_rs, d2_ss, d2_rs, d3_ss, d3_rs,
+    ld, g_ss, g_zs, y_ss, y_fs, y_l, y_r, y_o, a_ss, a_rs, yb_rs, d1_ss, d1_rs, d2_ss, d2_rs, d3_ss, d3_rs,
 ):
     v = lax.axis_index("vir")
     y = lax.axis_index("trip")
@@ -284,6 +284,10 @@
     for n in range(1, 3):
         loads[n].wait()
     tijp[...] = nt(tij[...], pm[...]).astype(BF)
+    out_t = pltpu.make_async_copy(tijp, tijp_hbm, ld.at[0])
+    out_p = pltpu.make_async_copy(pmt, pmt_hbm, ld.at[1])
+    out_t.start()
+    out_p.start()
 
     def c_part(c, carry):
         x = gk[c]
@@ -329,14 +333,14 @@
 
         lax.fori_loop(0, GROUPS, step, 0)
 
-    def send_b(src, dst, n):
+    def send_b(src, dst, n, rs):
         def step(s, c):
             g = lax.rem(grp + s, GROUPS)
             x = xb[:, rows_of(g), 256:512].reshape(L * GR, 256)
             m0, mixed = packed_b(x, xb[L - 1, rows_of(g), 0:256], pk, plast)
             src[slots_of(g), 0:48] = m0
             src[slots_of(g), 48:80] = mixed
-            send_group(src, dst, g, a_ss.at[n], a_rs.at[n])
+            send_group(src, dst, g, a_ss.at[n], rs)
             return c
 
         lax.fori_loop(0, GROUPS, step, 0)
@@ -379,7 +383,7 @@
         return carry
 
     lax.fori_loop(0, L, s_b, 0)
-    send_b(sb_send, sb_recv, 1)
+    send_b(sb_send, sb_recv, 1, a_rs.at[1])
 
     def b_part(i, carry):
         w[i, :, 0:V] = w[i, :, 0:V] + nt(tit[...], gj[i])
@@ -435,7 +439,7 @@
     lax.fori_loop(0, GROUPS, add_b, 0)
     e = lax.fori_loop(0, L, lambda i, e: weigh(i, rest, None, e), e)
     e = weigh(L - 1, first, late, e)
-    send_b(yb_send, yb_recv, 3)
+    send_b(yb_send, yb_recv, 3, yb_rs.at[grp])
 
     def gram_b(i, acc):
         x = xb[i, :, rest]
@@ -472,6 +476,28 @@
         gram.at[pl.ds(pl.multiple_of(piece * 64, 64), 64)], d1.at[piece], d1_rs
     ).start()
 
+    pltpu.make_async_copy(d1, d1, d1_rs).wait()
+    d2s[...] = jnp.sum(d1[...], axis=0)
+
+    def owner_send(o, c):
+        to = piece * 8 + o
+        src = d2s.at[pl.ds(pl.multiple_of(o * 8, 8), 8)]
+
+        @pl.when(to != v)
+        def _():
+            pltpu.make_async_remote_copy(
+                src_ref=src, dst_ref=d2.at[chip], send_sem=d2_ss, recv_sem=d2_rs,
+                device_id={"vir": to, "trip": y}, device_id_type=MESH,
+            ).start()
+
+        @pl.when(to == v)
+        def _():
+            pltpu.make_async_copy(src, d2.at[chip], d2_rs).start()
+
+        return c
+
+    lax.fori_loop(0, 8, owner_send, 0)
+
     all_of(ya_send, ya_recv, 2).wait_recv()
 
     def take_a(g, c):
@@ -488,31 +514,10 @@
         top = r.astype(BF)
         low = (r - top.astype(F32)).astype(BF)
         cs[c] = nt(x, tijp[:, 0:256]) + (nn(pmt[:, 0:256], top) + nn(pmt[:, 0:256], low))
+        pltpu.make_async_copy(cs.at[c], cs_hbm.at[c], ld.at[2]).start()
         return carry
 
-    lax.fori_loop(0, L - 1, out_first, 0)
-
-    pltpu.make_async_copy(d1, d1, d1_rs).wait()
-    d2s[...] = jnp.sum(d1[...], axis=0)
-
-    def owner_send(o, c):
-        to = piece * 8 + o
-        src = d2s.at[pl.ds(pl.multiple_of(o * 8, 8), 8)]
-
-        @pl.when(to != v)
-        def _():
-            pltpu.make_async_remote_copy(
-                src_ref=src, dst_ref=d2.at[chip], send_sem=d2_ss, recv_sem=d2_rs,
-                device_id={"vir": to, "trip": y}, device_id_type=MESH,
-            ).start()
-
-        @pl.when(to == v)
-        def _():
-            pltpu.make_async_copy(src, d2.at[chip], d2_rs).start()
-
-        return c
-
-    lax.fori_loop(0, 8, owner_send, 0)
+    lax.fori_loop(0, L, out_first, 0)
 
     is_owner = y == grp
 
@@ -522,17 +527,22 @@
             device_id={"vir": v, "trip": ty}, device_id_type=MESH,
         )
 
-    all_of(yb_send, yb_recv, 3).wait_recv()
-
-    def take_b(g, c):
+    def take_b(s, c):
+        g = group_at(s)
+        pltpu.make_async_copy(yb_recv.at[slots_of(g)], yb_recv.at[slots_of(g)], yb_rs.at[g]).wait()
         last = spread_b(yb_recv[slots_of(g), 0:48], yb_recv[slots_of(g), 48:80], tmp)
         o = nn(up[...], tmp[...]).reshape(L, GR, 256)
-        gk[:, rows_of(g), 256:V] = o[:, :, 0:192].astype(BF)
-        fix = gk[L - 1, rows_of(g), first].astype(F32) + nn(ulast[...], last)
-        gk[L - 1, rows_of(g), first] = fix.astype(BF)
+        xb[:, rows_of(g), first] = o.astype(BF)
+        xb[L - 1, rows_of(g), rest] = nn(ulast[...], last).astype(BF)
+        pltpu.make_async_copy(
+            xb.at[:, rows_of(g), first], xo_hbm.at[:, rows_of(g)], ld.at[3]
+        ).start()
+        pltpu.make_async_copy(
+            xb.at[L - 1, rows_of(g), rest], dx_hbm.at[rows_of(g)], ld.at[4]
+        ).start()
         return c
 
-    lax.fori_loop(0, GROUPS, take_b, 0)
+    lax.fori_loop(0, 2, take_b, 0)
 
     @pl.when(is_owner)
     def _():
@@ -541,29 +551,22 @@
         for dy in (1, 2, 3):
             fin_copy(lax.rem(y + dy, 4)).start()
 
-    def out_last(c, carry):
-        x = gk[c, :, 256:V]
-        r = tn(x, tij[...]).astype(BF)
-        gi[c] = (cs[c] + (nt(x, tijp[:, 256:V]) + nn(pmt[:, 256:V], r))).astype(BF)
-        pltpu.make_async_copy(gi.at[c], vvvo_hbm.at[0, c], ld.at[0]).start()
-        return carry
-
-    x = gk[L - 1]
-    r = tn(x, tij[...]).astype(BF)
-    gi[L - 1] = (nt(x, tijp[...]) + nn(pmt[...], r)).astype(BF)
-    pltpu.make_async_copy(gi.at[L - 1], vvvo_hbm.at[0, L - 1], ld.at[0]).start()
-    lax.fori_loop(0, L - 1, out_last, 0)
+    lax.fori_loop(2, GROUPS, take_b, 0)
 
     @pl.when(jnp.logical_not(is_owner))
     def _():
         fin_copy(y).wait_recv()
 
-    density_ref[...] = dfin[0:7, 0:V] * (1.0 / (V * V))
+    small[...] = dfin[...] * (1.0 / (V * V))
     sel = iota((1, 128), 1) == y
     es = jnp.sum(jnp.where(sel, dfin[7:8, 0:128], 0.0), axis=1, keepdims=True)
-    energy_ref[...] = jnp.broadcast_to(es * (1.0 / V**3), (8, 128))
-
-    pltpu.make_async_copy(gi, vvvo_hbm.at[0], ld.at[0]).wait()
+    small[7:8, 0:128] = jnp.broadcast_to(es * (1.0 / V**3), (1, 128))
+
+    out_t.wait()
+    out_p.wait()
+    pltpu.make_async_copy(cs, cs_hbm, ld.at[2]).wait()
+    pltpu.make_async_copy(xb.at[:, :, first], xo_hbm, ld.at[3]).wait()
+    pltpu.make_async_copy(xb.at[L - 1, :, rest], dx_hbm, ld.at[4]).wait()
     for h in range(2):
         part = g_send.at[0, pl.ds(0, N - 1)]
         pltpu.make_async_remote_copy(
@@ -609,21 +612,43 @@
             fin_copy(lax.rem(y + dy, 4)).wait_send()
 
 
+def finish(small, cs, xo, dx, tij, tijp, pmt, energy, density, vvvo):
+    c = pl.program_id(0)
+    x = xo[0, :, 0:192]
+    r = tn(x, tij[...]).astype(BF)
+    acc = cs[0] + (nt(x, tijp[:, 256:V]) + nn(pmt[:, 256:V], r))
+
+    @pl.when(c < L - 1)
+    def _():
+        vvvo[0, 0] = acc.astype(BF)
+
+    @pl.when(c == L - 1)
+    def _():
+        z = dx[...]
+        r = tn(z, tij[...]).astype(BF)
+        vvvo[0, 0] = (acc + (nt(z, tijp[:, 0:256]) + nn(pmt[:, 0:256], r))).astype(BF)
+        density[...] = small[0:7, 0:V]
+        energy[0] = jnp.sum(jnp.where(iota((1, 128), 1) == 0, small[7:8, 0:128], 0.0))
+
+
 def body(triplets, pair_integrals, k_integrals, pair_amplitudes, k_amplitudes, occ_energy, vir_energy):
     vm = pl.BlockSpec(memory_space=pltpu.VMEM)
     sm = pl.BlockSpec(memory_space=pltpu.SMEM)
     hbm = pl.BlockSpec(memory_space=pl.ANY)
     slab = pltpu.VMEM((L, V, V), BF)
     dma = pltpu.SemaphoreType.DMA
-    energy, density, vvvo = pl.pallas_call(
+    small, cs, xo, dx, tijp, pmt = pl.pallas_call(
         kernel,
         out_shape=(
-            jax.ShapeDtypeStruct((8, 128), F32),
-            jax.ShapeDtypeStruct((L, V), F32),
-            jax.ShapeDtypeStruct((1, L, V, V), BF),
+            jax.ShapeDtypeStruct((8, 512), F32),
+            jax.ShapeDtypeStruct((L, V, V), F32),
+            jax.ShapeDtypeStruct((L, V, 256), BF),
+            jax.ShapeDtypeStruct((V, 256), BF),
+            jax.ShapeDtypeStruct((V, V), BF),
+            jax.ShapeDtypeStruct((V, V), BF),
         ),
         in_specs=[sm, sm, sm, vm] + [hbm] * 7 + [vm] * 4,
-        out_specs=(vm, vm, hbm),
+        out_specs=(vm, hbm, hbm, hbm, hbm, hbm),
         scratch_shapes=[
             slab, slab, slab,
             pltpu.VMEM((V, V), BF),
@@ -656,7 +681,7 @@
             pltpu.VMEM((64, 512), F32),
             pltpu.VMEM((8, 512), F32),
             dma((8,)), dma((2,)), dma((8,)), dma((8,)), dma((8,)), dma((8,)), dma((8,)), dma((8,)),
-            dma((4,)), dma((4,)), dma, dma, dma, dma, dma, dma,
+            dma((4,)), dma((4,)), dma((4,)), dma, dma, dma, dma, dma, dma,
         ],
         compiler_params=pltpu.CompilerParams(
             collective_id=0, has_side_effects=True, vmem_limit_bytes=60 * 1024 * 1024
@@ -669,7 +694,32 @@
         jnp.asarray(pack_last(), BF), jnp.asarray(unpack_last(), BF),
         jnp.asarray(turn_pack_matrix(), BF), jnp.asarray(turn_unpack_matrix(), BF),
     )
-    return energy[0, 0:1], density, vvvo
+    whole = lambda shape: pl.BlockSpec(shape, lambda c: (0,) * len(shape))
+    return pl.pallas_call(
+        finish,
+        grid=(L,),
+        out_shape=(
+            jax.ShapeDtypeStruct((1,), F32),
+            jax.ShapeDtypeStruct((L, V), F32),
+            jax.ShapeDtypeStruct((1, L, V, V), BF),
+        ),
+        in_specs=[
+            whole((8, 512)),
+            pl.BlockSpec((1, V, V), lambda c: (c, 0, 0)),
+            pl.BlockSpec((1, V, 256), lambda c: (c, 0, 0)),
+            whole((V, 256)),
+            whole((V, V)),
+            whole((V, V)),
+            whole((V, V)),
+        ],
+        out_specs=(
+            pl.BlockSpec(memory_space=pltpu.SMEM),
+            whole((L, V)),
+            pl.BlockSpec((1, 1, V, V), lambda c: (0, c, 0, 0)),
+        ),
+        compiler_params=pltpu.CompilerParams(vmem_limit_bytes=60 * 1024 * 1024),
+        name="finish",
+    )(small, cs, xo, dx, pair_amplitudes, tijp, pmt)
 
 
 def solution(mesh):

time: 192 us -> 193 us (level)
  Pallas kernels: 185 us -> 192 us
  local copies, waits for them, and re-layouts: 6.41 us -> 0 us
    pallas_call x1 -> x2, Pallas kernels: 185 us -> 192 us  [the longest x1 181 us: body(): pl.pallas_call(kernel, out_shape=(jax.ShapeDtypeStruct((8, 512), F32), ja...]
    unnamed x2 -> x0, local copies, waits for them, and re-layouts: 5.22 us -> none
where the time goes in v4:
time: 193 us; the launch traced here: 192 us
  Pallas kernels  192 us (99%)
    pallas_call x1, Pallas kernels, body(): pl.pallas_call(kernel, out_shape=(jax.ShapeDtypeStruct((8, 512), F32), ja...  181 us
    pallas_call x1, Pallas kernels, body(): pl.pallas_call(finish, grid=(L,), out_shape=(jax.ShapeDtypeStruct((1,), F...  10.3 us

profile of v4, /device:TPU:1, one launch (start us, length us, event | category | flops | bytes accessed | tf_op | source)
XLA Modules:
  0.0 192.3 jit_solution(3239892927782999334)
XLA Ops:
  0.6 181.3 %triples.1 = (f32[8,512]{1,0:T(8,128)}, f32[7,448,448]{2,1,0:T(8,128)}, bf16[7,448,256]{2,1,0:T(8,128)(2,1)}, bf16[448,256]{1,0:T(8,128)(2,1)}, bf16[448,448]{1,0:T(8,128)(2,1)}, /*index=5*/bf16[448,448]{1,0:T(8,128)(2,1)}) custom-call(s32[1,3]{1,0:T(1,128)} %trip_ref.1, f32[120]{0:T(128)} %occ_ref.1, f32[448]{0:T(512)} %virs_ref.1, f32[1,448]{1,0:T(1,128)} %bitcast.1, ...), custom_call_target="tpu_custom_call" | custom-call | tf_op jit(solution)/shard_map/triples/pallas_call | solution.py:640
  181.9 10.3 %finish.1 = (f32[1]{0:T(128)}, f32[7,448]{1,0:T(8,128)}, bf16[1,7,448,448]{3,2,1,0:T(8,128)(2,1)}) custom-call(f32[8,512]{1,0:T(8,128)} %get-tuple-element.9.small, f32[7,448,448]{2,1,0:T(8,128)} %get-tuple-element.10.cs, bf16[7,448,256]{2,1,0:T(8,128)(2,1)} %get-tuple-element.11.xo, bf16[448,256]{1,0:T(8,128)(2,1)} %get-tuple-element.12.dx, ...), custom_call_target="tpu_custom_call" | custom-call | tf_op jit(solution)/shard_map/finish/pallas_call | solution.py:698

commit v5 on v4

--- a/solution.py
+++ b/solution.py
@@ -141,7 +141,7 @@
 
 def kernel(
     trip_ref, occ_ref, virs_ref, vir_ref, pair_hbm, k_hbm, tij_hbm, kamp_hbm, pk_hbm, up_hbm, row_hbm, plast, ulast, pkt, upt,
-    small, cs_hbm, xo_hbm, dx_hbm, tijp_hbm, pmt_hbm,
+    small, cs_hbm, r_hbm, rl_hbm, pmt_hbm,
     gi, gj, gk, tij, kamp, pk, up, rowm, cs, w, xb, tjt, tit, tjp, tijp, pm, pmt, vrow, tmp, tmpt,
     g_send, g_recv, sa_send, sa_recv, sb_send, sb_recv, ya_send, ya_recv, yb_send, yb_recv,
     gram, d1, d2, d2s, dfin,
@@ -284,9 +284,7 @@
     for n in range(1, 3):
         loads[n].wait()
     tijp[...] = nt(tij[...], pm[...]).astype(BF)
-    out_t = pltpu.make_async_copy(tijp, tijp_hbm, ld.at[0])
     out_p = pltpu.make_async_copy(pmt, pmt_hbm, ld.at[1])
-    out_t.start()
     out_p.start()
 
     def c_part(c, carry):
@@ -333,7 +331,7 @@
 
         lax.fori_loop(0, GROUPS, step, 0)
 
-    def send_b(src, dst, n, rs):
+    def send_b(src, dst, n, rs, start, stop):
         def step(s, c):
             g = lax.rem(grp + s, GROUPS)
             x = xb[:, rows_of(g), 256:512].reshape(L * GR, 256)
@@ -343,7 +341,7 @@
             send_group(src, dst, g, a_ss.at[n], rs)
             return c
 
-        lax.fori_loop(0, GROUPS, step, 0)
+        lax.fori_loop(start, stop, step, 0)
 
     def all_of(src, dst, n):
         return pltpu.make_async_remote_copy(
@@ -383,7 +381,7 @@
         return carry
 
     lax.fori_loop(0, L, s_b, 0)
-    send_b(sb_send, sb_recv, 1, a_rs.at[1])
+    send_b(sb_send, sb_recv, 1, a_rs.at[1], 0, GROUPS)
 
     def b_part(i, carry):
         w[i, :, 0:V] = w[i, :, 0:V] + nt(tit[...], gj[i])
@@ -439,7 +437,6 @@
     lax.fori_loop(0, GROUPS, add_b, 0)
     e = lax.fori_loop(0, L, lambda i, e: weigh(i, rest, None, e), e)
     e = weigh(L - 1, first, late, e)
-    send_b(yb_send, yb_recv, 3, yb_rs.at[grp])
 
     def gram_b(i, acc):
         x = xb[i, :, rest]
@@ -476,6 +473,8 @@
         gram.at[pl.ds(pl.multiple_of(piece * 64, 64), 64)], d1.at[piece], d1_rs
     ).start()
 
+    send_b(yb_send, yb_recv, 3, yb_rs.at[grp], 0, 2)
+
     pltpu.make_async_copy(d1, d1, d1_rs).wait()
     d2s[...] = jnp.sum(d1[...], axis=0)
 
@@ -498,6 +497,8 @@
 
     lax.fori_loop(0, 8, owner_send, 0)
 
+    send_b(yb_send, yb_recv, 3, yb_rs.at[grp], 2, GROUPS)
+
     all_of(ya_send, ya_recv, 2).wait_recv()
 
     def take_a(g, c):
@@ -514,7 +515,6 @@
         top = r.astype(BF)
         low = (r - top.astype(F32)).astype(BF)
         cs[c] = nt(x, tijp[:, 0:256]) + (nn(pmt[:, 0:256], top) + nn(pmt[:, 0:256], low))
-        pltpu.make_async_copy(cs.at[c], cs_hbm.at[c], ld.at[2]).start()
         return carry
 
     lax.fori_loop(0, L, out_first, 0)
@@ -531,18 +531,23 @@
         g = group_at(s)
         pltpu.make_async_copy(yb_recv.at[slots_of(g)], yb_recv.at[slots_of(g)], yb_rs.at[g]).wait()
         last = spread_b(yb_recv[slots_of(g), 0:48], yb_recv[slots_of(g), 48:80], tmp)
-        o = nn(up[...], tmp[...]).reshape(L, GR, 256)
-        xb[:, rows_of(g), first] = o.astype(BF)
-        xb[L - 1, rows_of(g), rest] = nn(ulast[...], last).astype(BF)
+        o = nn(up[...], tmp[...]).astype(BF)[:, 0:192]
+        t = tij[rows_of(g), :]
+        m = nt(o, tijp[:, 256:V]).reshape(L, GR, V)
+        cs[:, rows_of(g), :] = cs[:, rows_of(g), :] + m
+        for i in range(L):
+            w[i, 0:192, 0:V] = w[i, 0:192, 0:V] + tn(o[GR * i : GR * (i + 1)], t)
+        z = nn(ulast[...], last).astype(BF)
+        cs[L - 1, rows_of(g), :] = cs[L - 1, rows_of(g), :] + nt(z, tijp[:, 0:256])
+        w[0, 192:V, 0:V] = w[0, 192:V, 0:V] + tn(z, t)
         pltpu.make_async_copy(
-            xb.at[:, rows_of(g), first], xo_hbm.at[:, rows_of(g)], ld.at[3]
-        ).start()
-        pltpu.make_async_copy(
-            xb.at[L - 1, rows_of(g), rest], dx_hbm.at[rows_of(g)], ld.at[4]
+            cs.at[:, rows_of(g)], cs_hbm.at[:, rows_of(g)], ld.at[2]
         ).start()
         return c
 
-    lax.fori_loop(0, 2, take_b, 0)
+    w[:, 0:192, :] = jnp.zeros((L, 192, 512), F32)
+    w[0, 192:V, :] = jnp.zeros((256, 512), F32)
+    lax.fori_loop(0, 1, take_b, 0)
 
     @pl.when(is_owner)
     def _():
@@ -551,7 +556,13 @@
         for dy in (1, 2, 3):
             fin_copy(lax.rem(y + dy, 4)).start()
 
-    lax.fori_loop(2, GROUPS, take_b, 0)
+    lax.fori_loop(1, GROUPS, take_b, 0)
+    gi[:, 0:192, :] = w[:, 0:192, 0:V].astype(BF)
+    gk[0, 0:256, :] = w[0, 192:V, 0:V].astype(BF)
+    out_r = pltpu.make_async_copy(gi.at[:, pl.ds(0, 192)], r_hbm, ld.at[3])
+    out_l = pltpu.make_async_copy(gk.at[0, pl.ds(0, 256)], rl_hbm, ld.at[4])
+    out_r.start()
+    out_l.start()
 
     @pl.when(jnp.logical_not(is_owner))
     def _():
@@ -562,11 +573,10 @@
     es = jnp.sum(jnp.where(sel, dfin[7:8, 0:128], 0.0), axis=1, keepdims=True)
     small[7:8, 0:128] = jnp.broadcast_to(es * (1.0 / V**3), (1, 128))
 
-    out_t.wait()
     out_p.wait()
     pltpu.make_async_copy(cs, cs_hbm, ld.at[2]).wait()
-    pltpu.make_async_copy(xb.at[:, :, first], xo_hbm, ld.at[3]).wait()
-    pltpu.make_async_copy(xb.at[L - 1, :, rest], dx_hbm, ld.at[4]).wait()
+    out_r.wait()
+    out_l.wait()
     for h in range(2):
         part = g_send.at[0, pl.ds(0, N - 1)]
         pltpu.make_async_remote_copy(
@@ -612,11 +622,9 @@
             fin_copy(lax.rem(y + dy, 4)).wait_send()
 
 
-def finish(small, cs, xo, dx, tij, tijp, pmt, energy, density, vvvo):
+def finish(small, cs, r, rl, pmt, energy, density, vvvo):
     c = pl.program_id(0)
-    x = xo[0, :, 0:192]
-    r = tn(x, tij[...]).astype(BF)
-    acc = cs[0] + (nt(x, tijp[:, 256:V]) + nn(pmt[:, 256:V], r))
+    acc = cs[0] + nn(pmt[:, 256:V], r[0])
 
     @pl.when(c < L - 1)
     def _():
@@ -624,9 +632,7 @@
 
     @pl.when(c == L - 1)
     def _():
-        z = dx[...]
-        r = tn(z, tij[...]).astype(BF)
-        vvvo[0, 0] = (acc + (nt(z, tijp[:, 0:256]) + nn(pmt[:, 0:256], r))).astype(BF)
+        vvvo[0, 0] = (acc + nn(pmt[:, 0:256], rl[...])).astype(BF)
         density[...] = small[0:7, 0:V]
         energy[0] = jnp.sum(jnp.where(iota((1, 128), 1) == 0, small[7:8, 0:128], 0.0))
 
@@ -637,18 +643,17 @@
     hbm = pl.BlockSpec(memory_space=pl.ANY)
     slab = pltpu.VMEM((L, V, V), BF)
     dma = pltpu.SemaphoreType.DMA
-    small, cs, xo, dx, tijp, pmt = pl.pallas_call(
+    small, cs, r, rl, pmt = pl.pallas_call(
         kernel,
         out_shape=(
             jax.ShapeDtypeStruct((8, 512), F32),
             jax.ShapeDtypeStruct((L, V, V), F32),
-            jax.ShapeDtypeStruct((L, V, 256), BF),
-            jax.ShapeDtypeStruct((V, 256), BF),
-            jax.ShapeDtypeStruct((V, V), BF),
+            jax.ShapeDtypeStruct((L, 192, V), BF),
+            jax.ShapeDtypeStruct((256, V), BF),
             jax.ShapeDtypeStruct((V, V), BF),
         ),
         in_specs=[sm, sm, sm, vm] + [hbm] * 7 + [vm] * 4,
-        out_specs=(vm, hbm, hbm, hbm, hbm, hbm),
+        out_specs=(vm, hbm, hbm, hbm, hbm),
         scratch_shapes=[
             slab, slab, slab,
             pltpu.VMEM((V, V), BF),
@@ -706,10 +711,8 @@
         in_specs=[
             whole((8, 512)),
             pl.BlockSpec((1, V, V), lambda c: (c, 0, 0)),
-            pl.BlockSpec((1, V, 256), lambda c: (c, 0, 0)),
-            whole((V, 256)),
-            whole((V, V)),
-            whole((V, V)),
+            pl.BlockSpec((1, 192, V), lambda c: (c, 0, 0)),
+            whole((256, V)),
             whole((V, V)),
         ],
         out_specs=(
@@ -719,7 +722,7 @@
         ),
         compiler_params=pltpu.CompilerParams(vmem_limit_bytes=60 * 1024 * 1024),
         name="finish",
-    )(small, cs, xo, dx, pair_amplitudes, tijp, pmt)
+    )(small, cs, r, rl, pmt)
 
 
 def solution(mesh):

time: 193 us -> 190 us (0.984)
  Pallas kernels: 192 us -> 189 us
    pallas_call x1, Pallas kernels: 10.3 us -> 8.2 us  [body(): pl.pallas_call(finish, grid=(L,), out_shape=(jax.ShapeDtypeStruct((1,), F...]
where the time goes in v5:
time: 190 us
  Pallas kernels  189 us (99%)
    pallas_call x1, Pallas kernels, body(): pl.pallas_call(kernel, out_shape=(jax.ShapeDtypeStruct((8, 512), F32), ja...  181 us
    pallas_call x1, Pallas kernels, body(): pl.pallas_call(finish, grid=(L,), out_shape=(jax.ShapeDtypeStruct((1,), F...  8.2 us

profile of v5, /device:TPU:1, one launch (start us, length us, event | category | flops | bytes accessed | tf_op | source)
XLA Modules:
  0.0 190.1 jit_solution(15646286996932314639)
XLA Ops:
  0.6 181.2 %triples.1 = (f32[8,512]{1,0:T(8,128)}, f32[7,448,448]{2,1,0:T(8,128)}, bf16[7,192,448]{2,1,0:T(8,128)(2,1)}, bf16[256,448]{1,0:T(8,128)(2,1)}, bf16[448,448]{1,0:T(8,128)(2,1)}) custom-call(s32[1,3]{1,0:T(1,128)} %trip_ref.1, f32[120]{0:T(128)} %occ_ref.1, f32[448]{0:T(512)} %virs_ref.1, f32[1,448]{1,0:T(1,128)} %bitcast.1, ...), custom_call_target="tpu_custom_call" | custom-call | tf_op jit(solution)/shard_map/triples/pallas_call | solution.py:646
  181.9 8.2 %finish.1 = (f32[1]{0:T(128)}, f32[7,448]{1,0:T(8,128)}, bf16[1,7,448,448]{3,2,1,0:T(8,128)(2,1)}) custom-call(f32[8,512]{1,0:T(8,128)} %get-tuple-element.8.small, f32[7,448,448]{2,1,0:T(8,128)} %get-tuple-element.9.cs, bf16[7,192,448]{2,1,0:T(8,128)(2,1)} %get-tuple-element.10.r, bf16[256,448]{1,0:T(8,128)(2,1)} %get-tuple-element.11.rl, ...), custom_call_target="tpu_custom_call" | custom-call | tf_op jit(solution)/shard_map/finish/pallas_call | solution.py:703

commit v6 on v5

--- a/solution.py
+++ b/solution.py
@@ -275,6 +275,8 @@
                 at = pl.ds(pl.multiple_of(64 * (4 * h + p) + GD * g, GD), GD)
                 gj[q, at, :] = o[GD * (4 * q + p) : GD * (4 * q + p + 1), 0:V]
 
+    z_step(0, 0)
+
     pm[...] = jnp.where(
         iota((V, V), 1) == 7 * (iota((V, V), 0) & 63) + (iota((V, V), 0) >> 6), 1.0, 0.0
     ).astype(BF)
@@ -297,28 +299,25 @@
         w[i, :, 0:V] = nt(x, tjp[...]) + nt(tjt[...], nn(pm[...], x).astype(BF))
         return carry
 
-    lax.fori_loop(0, 3, c_part, 0)
-    z_step(0, 0)
-    lax.fori_loop(3, 6, c_part, 0)
     z_step(0, 1)
+    lax.fori_loop(0, 1, c_part, 0)
+    z_step(0, 2)
     y_step(0, 0)
-    lax.fori_loop(6, L, c_part, 0)
+    lax.fori_loop(1, 3, c_part, 0)
+    z_step(0, 3)
+    y_step(0, 1)
+    lax.fori_loop(3, 5, c_part, 0)
+    y_step(0, 2)
     for n in range(3, 8):
         loads[n].wait()
-    z_step(0, 2)
-    y_step(0, 1)
-    z_step(0, 3)
-    y_step(0, 2)
+    far_step(0, 0)
+    lax.fori_loop(5, L, c_part, 0)
+    y_step(0, 3)
     z_step(1, 0)
-    far_step(0, 0)
-    y_step(0, 3)
+    far_step(0, 1)
     z_step(1, 1)
-    far_step(0, 1)
     far_step(0, 2)
-    z_step(1, 2)
     far_step(0, 3)
-    z_step(1, 3)
-    y_step(1, 0)
 
     def send_a(src, dst, n):
         def step(s, c):
@@ -354,8 +353,11 @@
         return carry
 
     lax.fori_loop(0, L, s_a, 0)
+    z_step(1, 2)
     send_a(sa_send, sa_recv, 0)
 
+    z_step(1, 3)
+    y_step(1, 0)
     y_step(1, 1)
     tjt[...] = kamp[0, 1].astype(F32).T.astype(BF)
     tit[...] = kamp[0, 0].astype(F32).T.astype(BF)

time: 190 us -> 188 us (0.989)
  Pallas kernels: 189 us -> 187 us
    pallas_call x1, Pallas kernels: 181 us -> 179 us  [body(): pl.pallas_call(kernel, out_shape=(jax.ShapeDtypeStruct((8, 512), F32), ja...]
where the time goes in v6:
time: 188 us
  Pallas kernels  187 us (99%)
    pallas_call x1, Pallas kernels, body(): pl.pallas_call(kernel, out_shape=(jax.ShapeDtypeStruct((8, 512), F32), ja...  179 us
    pallas_call x1, Pallas kernels, body(): pl.pallas_call(finish, grid=(L,), out_shape=(jax.ShapeDtypeStruct((1,), F...  8.2 us

profile of v6, /device:TPU:1, one launch (start us, length us, event | category | flops | bytes accessed | tf_op | source)
XLA Modules:
  0.0 187.7 jit_solution(8441655700385369165)
XLA Ops:
  0.6 178.8 %triples.1 = (f32[8,512]{1,0:T(8,128)}, f32[7,448,448]{2,1,0:T(8,128)}, bf16[7,192,448]{2,1,0:T(8,128)(2,1)}, bf16[256,448]{1,0:T(8,128)(2,1)}, bf16[448,448]{1,0:T(8,128)(2,1)}) custom-call(s32[1,3]{1,0:T(1,128)} %trip_ref.1, f32[120]{0:T(128)} %occ_ref.1, f32[448]{0:T(512)} %virs_ref.1, f32[1,448]{1,0:T(1,128)} %bitcast.1, ...), custom_call_target="tpu_custom_call" | custom-call | tf_op jit(solution)/shard_map/triples/pallas_call | solution.py:648
  179.4 8.2 %finish.1 = (f32[1]{0:T(128)}, f32[7,448]{1,0:T(8,128)}, bf16[1,7,448,448]{3,2,1,0:T(8,128)(2,1)}) custom-call(f32[8,512]{1,0:T(8,128)} %get-tuple-element.8.small, f32[7,448,448]{2,1,0:T(8,128)} %get-tuple-element.9.cs, bf16[7,192,448]{2,1,0:T(8,128)(2,1)} %get-tuple-element.10.r, bf16[256,448]{1,0:T(8,128)(2,1)} %get-tuple-element.11.rl, ...), custom_call_target="tpu_custom_call" | custom-call | tf_op jit(solution)/shard_map/finish/pallas_call | solution.py:705
